TPU v7x, 32 devices: a whole 2x2x4 slice. The times are simulated.
32 devices in a mesh: dp: 2 (over y), tensor: 4 (over x, core), context: 4 (over z).
Axes of the slice: x: 2, y: 2, z: 4, core: 2. Of those that a mesh axis runs over, the one named last changes fastest.
Arguments:
- q_in: bfloat16 [2, 512, 4096], P('dp', 'context', 'tensor'), may hold values from -44 to 44
- k_in: bfloat16 [2, 512, 4096], P('dp', 'context', 'tensor'), may hold values from -6 to 6
- v_in: bfloat16 [2, 512, 4096], P('dp', 'context', 'tensor'), may hold values from -6 to 6
- short_filt: float32 [3, 7, 4096], P(None, None, 'tensor'), may hold values from -2 to 2
- long_filt: float32 [512, 4096], P('context', 'tensor'), may hold values from -1.1 to 1.1
- norm_gain: float32 [4096], P('tensor'), may hold values from 0.1 to 1.9
- grad_out: bfloat16 [2, 512, 4096], P('dp', 'context', 'tensor'), may hold values from -6 to 6
Outputs:
- mixed: bfloat16 [2, 512, 4096], P('dp', 'context', 'tensor')
- grad_inputs: bfloat16 [3, 2, 512, 4096], P(None, 'dp', 'context', 'tensor')
- grad_long: float32 [512, 4096], P('context', 'tensor')
- grad_short: float32 [3, 7, 4096], P(None, None, 'tensor')
All inputs are finite; a program needn't handle non-finite values.
Results may differ from a plain program's by a relative error of at most 0.00225.
Values may be sent and summed in bfloat16 or wider, within the bound.
A program may use at most 128 MiB of HBM per device.

v0:
```python
import math

import jax
import jax.numpy as jnp
from jax import lax
from jax.sharding import PartitionSpec as P

D = 4096
FILT = 7


EPS = 1e-06
HIGH = lax.Precision.HIGHEST


def passed_along(shard, axis, by):
    peers = lax.axis_size(axis)
    pairs = [(i, i + by) for i in range(peers) if 0 <= i + by < peers]
    return lax.ppermute(shard, axis, pairs)


def phases(first, second, modulus):
    product = first[:, None] * second[None, :] % modulus
    return product.astype(jnp.float32) * (2.0 * math.pi / modulus)


def block_table(block_len, sign):
    index = jnp.arange(block_len, dtype=jnp.int32)
    angle = phases(index, index, block_len)
    cosine = jnp.cos(angle)
    sine = jnp.sin(angle) * sign
    return jnp.stack([jnp.stack([cosine, sine]), jnp.stack([-sine, cosine])])


def forward_rows(values, modulus):
    count, block_len, width = values.shape
    ctx_size = lax.axis_size("context")
    sub_len = block_len // ctx_size
    spread = lax.all_to_all(
        values.reshape(count, 1, block_len, width),
        "context",
        split_axis=2,
        concat_axis=1,
        tiled=True,
    )
    freq = jnp.arange(2 * ctx_size, dtype=jnp.int32)
    place = (
        jnp.arange(ctx_size, dtype=jnp.int32)[:, None] * block_len
        + lax.axis_index("context") * sub_len
        + jnp.arange(sub_len, dtype=jnp.int32)[None, :]
    )
    angle = (freq[:, None, None] * place[None] % modulus).astype(jnp.float32) * (
        2.0 * math.pi / modulus
    )
    table = jnp.stack([jnp.cos(angle), -jnp.sin(angle)])
    turned = jnp.einsum("pkcs,ncsx->npksx", table, spread, precision=HIGH)
    moved = lax.all_to_all(turned, "context", split_axis=2, concat_axis=3, tiled=True)
    return jnp.einsum("pqmb,nqjbx->npjmx", block_table(block_len, 1.0), moved, precision=HIGH)


def inverse_rows(spec, modulus):
    rows = spec.shape[2]
    block_len = spec.shape[3]
    ctx_size = lax.axis_size("context")
    index = jnp.arange(block_len, dtype=jnp.int32)
    freq = 2 * lax.axis_index("context") + jnp.arange(rows, dtype=jnp.int32)
    total = freq[:, None, None] + 2 * ctx_size * index[None, :, None]
    angle = (total * index[None, None, :] % modulus).astype(jnp.float32) * (2.0 * math.pi / modulus)
    cosine = jnp.cos(angle)
    sine = jnp.sin(angle)
    table = jnp.stack([jnp.stack([cosine, -sine]), jnp.stack([sine, cosine])])
    turned = jnp.einsum("pqjmb,nqjmx->npjbx", table, spec, precision=HIGH)
    moved = lax.all_to_all(turned, "context", split_axis=3, concat_axis=2, tiled=True)
    outer = phases(
        jnp.arange(ctx_size, dtype=jnp.int32),
        jnp.arange(2 * ctx_size, dtype=jnp.int32),
        2 * ctx_size,
    )
    real_table = jnp.stack([jnp.cos(outer), -jnp.sin(outer)])
    values = jnp.einsum("qck,nqksx->ncsx", real_table, moved, precision=HIGH) / modulus
    back = lax.all_to_all(values, "context", split_axis=1, concat_axis=2, tiled=True)
    return back.reshape(back.shape[0], back.shape[2], back.shape[3])


def shards(q_in, k_in, v_in, short_filt, long_filt, norm_gain, grad_out):
    block_len = q_in.shape[1]
    channels = q_in.shape[2]
    edge_rows = FILT - 1
    modulus = 2 * lax.axis_size("context") * block_len
    branches = jnp.stack([q_in[0], k_in[0], v_in[0]])
    before = passed_along(branches[:, block_len - edge_rows :], "context", 1)
    inputs = jnp.concatenate([before, branches], 1).astype(jnp.float32)
    shorts = jnp.zeros((3, block_len, channels), jnp.float32)
    for lag in range(FILT):
        shorts = (
            shorts
            + short_filt[:, lag][:, None, :]
            * inputs[:, edge_rows - lag : edge_rows - lag + block_len]
        )
    q_short = shorts[0]
    k_short = shorts[1]
    v_short = shorts[2]
    kv_prod = k_short * v_short
    spectra = forward_rows(jnp.stack([kv_prod, long_filt]), modulus)
    kv_real, kv_imag = (spectra[0, 0], spectra[0, 1])
    filt_real, filt_imag = (spectra[1, 0], spectra[1, 1])
    conv_spec = jnp.stack(
        [kv_real * filt_real - kv_imag * filt_imag, kv_real * filt_imag + kv_imag * filt_real]
    )[None]
    conv = inverse_rows(conv_spec, modulus)[0]
    y_out = q_short * conv
    squares = lax.psum(jnp.sum(y_out * y_out, axis=-1), "tensor")
    rms = jnp.sqrt(squares / D + EPS)[:, None]
    mixed = (y_out / rms * norm_gain).astype(jnp.bfloat16)[None]
    grad_z = grad_out[0].astype(jnp.float32) * norm_gain
    prods = lax.psum(jnp.sum(grad_z * y_out, axis=-1), "tensor")[:, None]
    grad_y = grad_z / rms - y_out * prods / (D * rms**3)
    dconv = grad_y * q_short
    grad_q = grad_y * conv
    grad_spec = forward_rows(dconv[None], modulus)[0]
    grad_real = grad_spec[0]
    grad_imag = grad_spec[1]
    dkv_spec = jnp.stack(
        [
            filt_real * grad_real + filt_imag * grad_imag,
            filt_real * grad_imag - filt_imag * grad_real,
        ]
    )
    dfilt_spec = jnp.stack(
        [kv_real * grad_real + kv_imag * grad_imag, kv_real * grad_imag - kv_imag * grad_real]
    )
    results = inverse_rows(jnp.stack([dkv_spec, dfilt_spec]), modulus)
    dkv = results[0]
    dfilt_local = results[1]
    grads = jnp.stack([grad_q, dkv * v_short, dkv * k_short])
    after = passed_along(grads[:, :edge_rows].astype(jnp.bfloat16), "context", -1).astype(
        jnp.float32
    )
    extended = jnp.concatenate([grads, after], 1)
    grad_inputs = jnp.zeros((3, block_len, channels), jnp.float32)
    for lag in range(FILT):
        grad_inputs = (
            grad_inputs + short_filt[:, lag][:, None, :] * extended[:, lag : lag + block_len]
        )
    short_local = jnp.stack(
        [
            jnp.sum(grads * inputs[:, edge_rows - lag : edge_rows - lag + block_len], axis=1)
            for lag in range(FILT)
        ],
        1,
    )
    scale = 1.0 / math.sqrt(lax.axis_size("dp") * block_len * lax.axis_size("context"))
    grad_long = lax.psum(dfilt_local, "dp") * scale
    grad_short = lax.psum(short_local, ("dp", "context")) * scale
    return (mixed, grad_inputs.astype(jnp.bfloat16)[:, None], grad_long, grad_short)


def solution(mesh):
    in_specs = (
        P("dp", "context", "tensor"),
        P("dp", "context", "tensor"),
        P("dp", "context", "tensor"),
        P(None, None, "tensor"),
        P("context", "tensor"),
        P("tensor"),
        P("dp", "context", "tensor"),
    )
    out_specs = (
        P("dp", "context", "tensor"),
        P(None, "dp", "context", "tensor"),
        P("context", "tensor"),
        P(None, None, "tensor"),
    )
    return jax.shard_map(shards, mesh=mesh, in_specs=in_specs, out_specs=out_specs, check_vma=False)
```

profile of v0, /device:TPU:0, one launch (start us, length us, event | category | flops | bytes accessed | tf_op | source)
XLA Modules:
  0.0 624.9 jit_solution(16772576711227980022)
XLA Ops:
  7.2 1.0 constant_dynamic-update-slice_fusion.2
  8.2 1.0 constant_dynamic-update-slice_fusion.1
  9.2 1.0 constant_dynamic-update-slice_fusion
  10.1 4.9 collective-permute-start
  15.3 1.5 collective-permute-done
  17.1 1.3 multiply_add_fusion
  18.5 1.0 copy-done.18
  19.5 1.8 copy.91
  21.3 5.6 all-to-all-start
  27.8 23.8 %all-to-all-done = f32[2,1,128,1024]{3,0,1,2:T(2,128)} async-done(((f32[2,1,128,1024]{3,0,1,2:T(2,128)}), f32[2,1,128,1024]{3,0,1,2:T(2,128)}, u32[]{:S(2)}, u32[]{:S(2)}) %all-to-all-start) | async-done | bytes 1048608 | tf_op jit(solution)/shard_map/all_to_all | solution.py:39
  51.6 5.3 convolution_bitcast_fusion
  56.9 5.3 copy.95
  62.2 5.1 all-to-all-start.1
  67.8 0.7 maximum_bitcast_fusion.7
  69.2 0.7 maximum_bitcast_fusion.5
  70.0 89.8 %all-to-all-done.1 = f32[2,2,8,32,1024]{4,1,0,3,2:T(2,128)} async-done(((f32[2,2,8,32,1024]{4,1,0,3,2:T(2,128)}), f32[2,2,8,32,1024]{4,1,0,3,2:T(2,128)}, u32[]{:S(2)}, u32[]{:S(2)}) %all-to-all-start.1) | async-done | bytes 4194336 | tf_op jit(solution)/shard_map/all_to_all | solution.py:57
  159.7 4.6 copy.96
  165.3 7.1 %fusion.4 = f32[2,2,2,128,1024]{3,4,1,2,0:T(8,128)S(1)} fusion(f32[2,2,2,128,1024,1]{4,3,2,1,0,5:T(8,128)S(1)} %bitcast.282, f32[1,2,128,128]{3,2,1,0:T(8,128)S(1)} %copy-done.16, f32[1,2,128,128]{3,2,1,0:T(8,128)S(1)} %copy-done.14), kind=kOutput, calls=%fused_computation.5 | convolution fusion | flops 3221291008 | bytes 8650752 | tf_op jit(solution)/shard_map/pqmb,nqjbx->npjmx/dot_general | solution.py:58
  172.7 1.7 copy-done
  174.4 3.8 fusion.12
  178.2 4.2 copy.106
  182.4 4.5 all-to-all-start.2
  187.5 47.1 %all-to-all-done.2 = f32[1,2,2,128,1024]{4,1,2,0,3:T(2,128)} async-done(((f32[1,2,2,128,1024]{4,1,2,0,3:T(2,128)}), f32[1,2,2,128,1024]{4,1,2,0,3:T(2,128)}, u32[]{:S(2)}, u32[]{:S(2)}) %all-to-all-start.2) | async-done | bytes 2097184 | tf_op jit(solution)/shard_map/all_to_all | solution.py:73
  234.6 2.8 copy.107
  237.4 3.0 copy.108
  240.4 3.8 reshape.785
  244.2 2.8 fusion.25
  247.3 16.4 %all_to_all.105 = f32[1,4,32,1024]{3,2,0,1:T(8,128)S(1)} all-to-all(f32[1,4,32,1024]{3,2,0,1:T(8,128)S(1)} %copy.109), channel_id=1, replica_groups=mesh['dp'=2,'tensor'=4,'context'=4] {'context'}, dimensions={1} | all-to-all | bytes 1048576 | tf_op jit(solution)/shard_map/all_to_all | solution.py:81
  263.7 0.8 copy-done.8
  264.5 0.7 fusion.41
  265.3 6.3 %all-reduce = (f32[128]{0:T(128)}, f32[128]{0:T(128)}) all-reduce(f32[128]{0:T(128)} %get-tuple-element.24, f32[128]{0:T(128)} %get-tuple-element.23), channel_id=1, replica_groups=mesh['dp'=2,'tensor'=4,'context'=4] {'tensor'}, use_global_device_ids=true, to_apply=%region_1.2 | all-reduce | flops 256 | bytes 2048 | tf_op jit(solution)/shard_map/psum | solution.py:112
  271.6 0.7 fusion.83
  272.9 1.3 fusion.45
  274.2 1.3 copy.110
  275.5 4.1 all-to-all-start.4
  279.9 1.5 copy.112
  281.4 13.1 %all-to-all-done.4 = f32[1,1,128,1024]{3,1,0,2:T(1,128)} async-done(((f32[1,1,128,1024]{3,1,0,2:T(1,128)}), f32[1,1,128,1024]{3,1,0,2:T(1,128)}, u32[]{:S(2)}, u32[]{:S(2)}) %all-to-all-start.4) | async-done | bytes 524320 | tf_op jit(solution)/shard_map/all_to_all | solution.py:39
  294.5 1.1 copy.171
  295.7 2.9 convolution_bitcast_fusion.1
  298.6 1.6 copy.113
  300.2 50.2 %all_to_all.106 = f32[1,2,8,32,1024]{4,1,3,0,2:T(2,128)S(1)} all-to-all(f32[1,2,8,32,1024]{4,1,3,0,2:T(2,128)S(1)} %copy.113), channel_id=1, replica_groups=mesh['dp'=2,'tensor'=4,'context'=4] {'context'}, dimensions={2} | all-to-all | bytes 4194304 | tf_op jit(solution)/shard_map/all_to_all | solution.py:57
  350.4 0.7 copy.114
  352.1 3.6 convolution_bitcast_fusion.2
  356.5 0.8 copy-done.11
  357.3 5.0 fusion.7
  362.3 7.3 %copy.122 = f32[2,2,2,128,1024]{4,1,0,2,3:T(2,128)} copy(f32[2,2,2,128,1024]{3,4,1,0,2:T(8,128)} %fusion.7) | data formatting | bytes 8388608 | tf_op jit(solution)/shard_map/pqjmb,nqjmx->npjbx/transpose | solution.py:72
  369.6 96.2 %all_to_all.107 = f32[2,2,2,128,1024]{4,1,0,2,3:T(2,128)S(1)} all-to-all(f32[2,2,2,128,1024]{4,1,0,2,3:T(2,128)} %copy.122), channel_id=1, replica_groups=mesh['dp'=2,'tensor'=4,'context'=4] {'context'}, dimensions={3} | all-to-all | bytes 8388608 | tf_op jit(solution)/shard_map/all_to_all | solution.py:73
  465.8 2.4 copy.123
  468.2 5.3 copy.124
  473.5 6.1 all_to_all.95
  479.6 4.5 fusion.23
  484.8 27.6 %all_to_all.108 = f32[2,4,32,1024]{3,2,0,1:T(8,128)S(1)} all-to-all(f32[2,4,32,1024]{3,2,0,1:T(8,128)S(1)} %copy.125), channel_id=1, replica_groups=mesh['dp'=2,'tensor'=4,'context'=4] {'context'}, dimensions={1} | all-to-all | bytes 2097152 | tf_op jit(solution)/shard_map/all_to_all | solution.py:81
  512.4 0.9 fusion.91
  513.3 1.0 fusion.38
  514.3 1.5 multiply_reduce_fusion
  516.7 1.5 pad_maximum_fusion.1
  518.2 1.3 collective-permute-start.1
  519.6 4.8 collective-permute-done.1
  525.2 2.2 fusion.35
  527.4 57.6 %all-reduce.6.cloned.1.call-done = f32[3,7,1024]{2,0,1:T(4,128)} async-done(((f32[3,7,1024]{2,0,1:T(4,128)}), f32[3,7,1024]{2,0,1:T(4,128)}) %all-reduce.6.cloned.1.call-update) | async-done | bytes 86032 | tf_op jit(solution)/shard_map/psum | solution.py:154
  585.0 0.9 broadcast_multiply_fusion.1
  585.9 0.7 copy.129
  586.6 29.2 %all-reduce.4.cloned.1.call-done = f32[128,1024]{1,0:T(8,128)} async-done(((f32[128,1024]{1,0:T(8,128)}), f32[128,1024]{1,0:T(8,128)}) %all-reduce.4.cloned.1.call-update) | async-done | bytes 524304 | tf_op jit(solution)/shard_map/psum | solution.py:153
  615.8 1.9 broadcast_multiply_fusion
  (116 shorter events, 9.5 us)
Async XLA Ops:
  7.2 7.9 %copy-start.28 = (f32[3,7,1024]{2,1,0:T(8,128)S(1)}, f32[3,7,1024]{2,1,0:T(8,128)}, u32[]{:S(2)}) copy-start(f32[3,7,1024]{2,1,0:T(8,128)} %param.10) | copy-start | bytes 258052
  10.1 6.7 %collective-permute-start = (bf16[3,6,1024]{2,1,0:T(8,128)(2,1)S(1)}, bf16[3,6,1024]{2,1,0:T(8,128)(2,1)S(1)}, u32[]{:S(2)}, u32[]{:S(2)}) collective-permute-start(bf16[3,6,1024]{2,1,0:T(8,128)(2,1)S(1)} %slice.152), channel_id=1, source_target_pairs={{0,1},{1,2},{2,3},{4,5},{5,6},{6,7},{8,9},{9,10},{10,11},{12,13},{... | collective-permute-start | bytes 110600 | tf_op jit(solution)/shard_map/ppermute | solution.py:19
  15.2 3.1 copy-start.20
  15.2 3.1 copy-start.22
  15.2 3.1 copy-start.24
  15.3 3.1 copy-start.26
  18.4 1.0 copy-start.18
  21.3 30.3 %all-to-all-start = ((f32[2,1,128,1024]{3,0,1,2:T(2,128)}), f32[2,1,128,1024]{3,0,1,2:T(2,128)}, u32[]{:S(2)}, u32[]{:S(2)}) async-start(f32[2,1,128,1024]{3,0,1,2:T(2,128)} %copy.91), calls=%async_computation | async-start | bytes 2097152 | tf_op jit(solution)/shard_map/all_to_all | solution.py:39
  62.2 97.5 %all-to-all-start.1 = ((f32[2,2,8,32,1024]{4,1,0,3,2:T(2,128)}), f32[2,2,8,32,1024]{4,1,0,3,2:T(2,128)}, u32[]{:S(2)}, u32[]{:S(2)}) async-start(f32[2,2,8,32,1024]{4,1,0,3,2:T(2,128)} %copy.95), calls=%async_computation.1 | async-start | bytes 8388608 | tf_op jit(solution)/shard_map/all_to_all | solution.py:57
  164.3 0.9 copy-start.14
  164.3 1.0 copy-start.16
  172.4 2.0 copy-start
  172.4 2.0 copy-start.10
  182.4 52.2 %all-to-all-start.2 = ((f32[1,2,2,128,1024]{4,1,2,0,3:T(2,128)}), f32[1,2,2,128,1024]{4,1,2,0,3:T(2,128)}, u32[]{:S(2)}, u32[]{:S(2)}) async-start(f32[1,2,2,128,1024]{4,1,2,0,3:T(2,128)} %copy.106), calls=%async_computation.2 | async-start | bytes 4194304 | tf_op jit(solution)/shard_map/all_to_all | solution.py:73
  247.0 17.5 %copy-start.12 = (bf16[1,128,1024]{2,1,0:T(8,128)(2,1)S(1)}, bf16[1,128,1024]{2,1,0:T(8,128)(2,1)}, u32[]{:S(2)}) copy-start(bf16[1,128,1024]{2,1,0:T(8,128)(2,1)} %param.13) | copy-start | bytes 786436
  247.0 17.5 %copy-start.29 = (f32[1024]{0:T(1024)S(1)}, f32[1024]{0:T(1024)}, u32[]{:S(2)}) copy-start(f32[1024]{0:T(1024)} %param.12) | copy-start | bytes 12292
  263.7 0.8 copy-start.8
  272.3 0.6 copy-start.34
  272.3 0.6 copy-start.36
  275.5 19.0 %all-to-all-start.4 = ((f32[1,1,128,1024]{3,1,0,2:T(1,128)}), f32[1,1,128,1024]{3,1,0,2:T(1,128)}, u32[]{:S(2)}, u32[]{:S(2)}) async-start(f32[1,1,128,1024]{3,1,0,2:T(1,128)} %copy.110), calls=%async_computation.4 | async-start | bytes 1048576 | tf_op jit(solution)/shard_map/all_to_all | solution.py:39
  279.7 305.3 %all-reduce.6.cloned.1.call-start = ((), (), s32[]{:S(2)}) async-start(), calls=%async_computation.9 | async-start | bytes 229376 | tf_op jit(solution)/shard_map/psum | solution.py:154
  351.1 0.9 copy-start.15
  351.1 1.0 copy-start.17
  352.1 3.6 copy-start.1
  356.4 1.0 copy-start.11
  473.5 6.1 copy-start.31
  473.5 6.1 copy-start.32
  484.7 28.6 %copy-start.9 = (f32[1,4,32,1024]{3,2,0,1:T(8,128)S(1)}, f32[1,4,32,1024]{3,2,0,1:T(8,128)}, u32[]{:S(2)}) copy-start(f32[1,4,32,1024]{3,2,0,1:T(8,128)} %copy-done.8) | copy-start | bytes 1572868
  484.7 28.6 %copy-start.13 = (bf16[1,128,1024]{2,1,0:T(8,128)(2,1)S(1)}, bf16[1,128,1024]{2,1,0:T(8,128)(2,1)}, u32[]{:S(2)}) copy-start(bf16[1,128,1024]{2,1,0:T(8,128)(2,1)} %param.13) | copy-start | bytes 786436
  484.7 28.6 %copy-start.30 = (f32[1024]{0:T(1024)S(1)}, f32[1024]{0:T(1024)}, u32[]{:S(2)}) copy-start(f32[1024]{0:T(1024)} %param.12) | copy-start | bytes 12292
  484.7 28.6 %copy-start.33 = (f32[128]{0:T(128)S(1)}, f32[128]{0:T(128)}, u32[]{:S(2)}) copy-start(f32[128]{0:T(128)} %get-tuple-element.26) | copy-start | bytes 1540
  484.8 28.6 %copy-start.35 = (f32[128]{0:T(128)S(1)}, f32[128]{0:T(128)}, u32[]{:S(2)}) copy-start(f32[128]{0:T(128)} %copy-done.34) | copy-start | bytes 1540
  484.8 28.6 %copy-start.37 = (f32[128]{0:T(128)S(1)}, f32[128]{0:T(128)}, u32[]{:S(2)}) copy-start(f32[128]{0:T(128)} %copy-done.36) | copy-start | bytes 1540
  514.3 1.5 copy-start.2
  514.3 1.5 copy-start.4
  514.3 1.5 copy-start.6
  515.9 8.4 %copy-start.3 = (f32[1,128,1024]{2,1,0:T(8,128)S(1)}, f32[1,128,1024]{2,1,0:T(8,128)}, u32[]{:S(2)}) copy-start(f32[1,128,1024]{2,1,0:T(8,128)} %copy-done.2) | copy-start | bytes 1572868
  515.9 8.4 %copy-start.5 = (f32[1,128,1024]{2,1,0:T(8,128)S(1)}, f32[1,128,1024]{2,1,0:T(8,128)}, u32[]{:S(2)}) copy-start(f32[1,128,1024]{2,1,0:T(8,128)} %copy-done.4) | copy-start | bytes 1572868
  516.0 8.4 %copy-start.7 = (f32[1,128,1024]{2,1,0:T(8,128)S(1)}, f32[1,128,1024]{2,1,0:T(8,128)}, u32[]{:S(2)}) copy-start(f32[1,128,1024]{2,1,0:T(8,128)} %copy-done.6) | copy-start | bytes 1572868
  516.0 0.6 copy-start.19
  516.7 99.1 %all-reduce.4.cloned.1.call-start = ((), (), s32[]{:S(2)}) async-start(), calls=%async_computation.8 | async-start | bytes 1048576 | tf_op jit(solution)/shard_map/psum | solution.py:153
  518.2 6.1 collective-permute-start.1
  524.4 0.7 copy-start.21
  524.4 0.7 copy-start.23
  524.4 0.7 copy-start.25
  524.4 0.7 copy-start.27
Sparse Core Ops, SparseCore 0:
  516.8 68.1 all-reduce.5
  587.4 28.3 all-reduce.3
where the time goes:
time: 634 us; the launch traced here: 625 us
  waiting for transfers between devices  267 us (42%)
  blocking collectives  197 us (31%)
  local copies, waits for them, and re-layouts  66.6 us (11%)
  matrix products  35 us (6%)
  starting transfers between devices  25.7 us (4%)
  other arithmetic  18.7 us (3%)
  between operations  15.2 us (2%)
    all_to_all x1, blocking collectives, inverse_rows(): lax.all_to_all(turned, 'context', split_axis=3, concat_axis=2, tiled=True)  96.2 us
    all_to_all x1, waiting for transfers between devices, forward_rows(): lax.all_to_all(turned, 'context', split_axis=2, concat_axis=3, tiled=True)  89.8 us
    psum x1, waiting for transfers between devices, shards(): grad_short = lax.psum(short_local, ('dp', 'context')) * scale  57.6 us
    all_to_all x1, blocking collectives, forward_rows(): lax.all_to_all(turned, 'context', split_axis=2, concat_axis=3, tiled=True)  50.2 us
    all_to_all x1, waiting for transfers between devices, inverse_rows(): lax.all_to_all(turned, 'context', split_axis=3, concat_axis=2, tiled=True)  47.1 us
    all_to_all x2, blocking collectives, inverse_rows(): lax.all_to_all(values, 'context', split_axis=1, concat_axis=2, tiled=True)  44 us
    all_to_all x2, waiting for transfers between devices, forward_rows(): lax.all_to_all(values.reshape(count, 1, block_len, width), 'context', spl...  36.9 us
    psum x1, waiting for transfers between devices, shards(): grad_long = lax.psum(dfilt_local, 'dp') * scale  29.2 us
  transfers between devices with their start and end apart: 8, of which 8 were waited for; matrix products, arithmetic and copies ran while one was open for 2% of the time, Pallas kernels for 0%

commit v1 on v0

--- a/solution.py
+++ b/solution.py
@@ -1,8 +1,12 @@
+import functools
 import math
 
 import jax
 import jax.numpy as jnp
+import numpy as np
 from jax import lax
+from jax.experimental import pallas as pl
+from jax.experimental.pallas import tpu as pltpu
 from jax.sharding import PartitionSpec as P
 
 D = 4096
@@ -154,6 +158,547 @@
     grad_short = lax.psum(short_local, ("dp", "context")) * scale
     return (mixed, grad_inputs.astype(jnp.bfloat16)[:, None], grad_long, grad_short)
 
+MESH = pl.DeviceIdType.MESH
+F32 = jnp.float32
+BF16 = jnp.bfloat16
+PAD = 16
+ROWS = 32
+
+
+def split_table(table):
+    high = table.astype(jnp.bfloat16)
+    low = (table - high.astype(np.float64)).astype(jnp.bfloat16)
+    return high, low
+
+
+def odd_tables(seq):
+    freq = 2 * np.arange(seq)[:, None] + 1
+    angle = (freq * np.arange(seq)[None, :] % (4 * seq)) * (np.pi / (2 * seq))
+    forward = np.concatenate([np.cos(angle), -np.sin(angle)], 0)
+    return split_table(forward) + split_table(np.ascontiguousarray(forward.T) / seq)
+
+
+def halves(values):
+    high = values.astype(BF16)
+    return high, (values - high.astype(F32)).astype(BF16)
+
+
+def dot(a, b):
+    return jnp.dot(a, b, preferred_element_type=F32)
+
+
+def dot3(ah, al, bh, bl):
+    return dot(ah, bh) + (dot(ah, bl) + dot(al, bh))
+
+
+def operator_kernel(
+    model_width,
+    total_rows,
+    q_in,
+    k_in,
+    v_in,
+    g_in,
+    f_in,
+    short_filt,
+    gain_in,
+    wh_in,
+    wl_in,
+    vh_in,
+    vl_in,
+    mixed,
+    grad_inputs,
+    grad_long,
+    grad_short,
+    branch,
+    filt,
+    wh,
+    wl,
+    vh,
+    vl,
+    shorts,
+    op_h,
+    op_l,
+    spec_kv,
+    spec_f,
+    spec_g,
+    prod_h,
+    prod_l,
+    conv,
+    y_buf,
+    sums,
+    stats,
+    grads,
+    dfilt,
+    dfilt_in,
+    dfilt_sum,
+    short_sum,
+    sent,
+    in_send,
+    in_recv,
+    in_local,
+    hop_send,
+    hop_recv,
+    tab_sem,
+    st_send,
+    st_recv,
+    out_send,
+    out_recv,
+    out_local,
+    df_send,
+    df_recv,
+    gl_send,
+    gl_recv,
+    gl_local,
+    fw_send,
+    fw_recv,
+    sh_send,
+    sh_recv,
+    gs_send,
+    gs_recv,
+    gs_local,
+):
+    ctx = lax.axis_size("context")
+    tens = lax.axis_size("tensor")
+    dp = lax.axis_index("dp")
+    me = lax.axis_index("context")
+    row = lax.axis_index("tensor")
+    block = q_in.shape[0]
+    seq = block * ctx
+    width = branch.shape[2]
+    half = width // 2
+    taps = short_filt.shape[1]
+    other = {"dp": 1 - dp}
+
+    def peer(off):
+        return lax.rem(me + off, ctx)
+
+    def source(off):
+        return lax.rem(me + ctx - off, ctx)
+
+    def rows_of(p):
+        return pl.ds(pl.multiple_of(p * block, block), block)
+
+    def cols_of(p):
+        return pl.ds(pl.multiple_of(p * width, width), width)
+
+    def half_cols(p, h):
+        return pl.ds(pl.multiple_of(p * width + h * half, half), half)
+
+    def remote(src, dst, send, recv, device):
+        copy = pltpu.make_async_remote_copy(
+            src_ref=src, dst_ref=dst, send_sem=send, recv_sem=recv, device_id=device, device_id_type=MESH
+        )
+        copy.start()
+        return copy
+
+    def local(src, dst, sem):
+        copy = pltpu.make_async_copy(src, dst, sem)
+        copy.start()
+        return copy
+
+    tables = [
+        local(src, dst, tab_sem.at[n])
+        for n, (src, dst) in enumerate([(wh_in, wh), (wl_in, wl), (vh_in, vh), (vl_in, vl)])
+    ]
+
+    barrier = pltpu.get_barrier_semaphore()
+    near = [(a, b) for a in range(tens) for b in range(ctx) if a + b > 0]
+    for a, b in near:
+        pl.semaphore_signal(
+            barrier,
+            inc=1,
+            device_id={"tensor": lax.rem(row + a, tens), "context": peer(b)},
+            device_id_type=MESH,
+        )
+    pl.semaphore_signal(barrier, inc=1, device_id=other, device_id_type=MESH)
+    pl.semaphore_wait(barrier, len(near) + 1)
+
+    f_copies = [
+        remote(
+            f_in.at[:, half_cols(peer(off), dp)],
+            filt.at[dp, rows_of(me), :],
+            in_send.at[4, off],
+            in_recv.at[4, off],
+            {"context": peer(off)},
+        )
+        for off in range(1, ctx)
+    ]
+    f_own = local(f_in.at[:, half_cols(me, dp)], filt.at[dp, rows_of(me), :], in_local.at[4])
+    land = pl.ds(pl.multiple_of(PAD + me * block, PAD), block)
+    arrivals = {}
+    for n, ref in ((1, k_in), (2, v_in), (0, q_in), (3, g_in)):
+        arrivals[n] = [
+            remote(
+                ref.at[:, cols_of(peer(off))],
+                branch.at[n, land, :],
+                in_send.at[n, off],
+                in_recv.at[n, off],
+                {"context": peer(off)},
+            )
+            for off in range(1, ctx)
+        ]
+        arrivals[n].append(local(ref.at[:, cols_of(me)], branch.at[n, land, :], in_local.at[n]))
+
+    def arrived(n):
+        for copy in arrivals[n][:-1]:
+            copy.wait_recv()
+        arrivals[n][-1].wait()
+
+    branch[:, :PAD, :] = jnp.zeros((4, PAD, width), BF16)
+    grads[:, seq:, :] = jnp.zeros((3, 8, width), F32)
+    short_sum[...] = jnp.zeros_like(short_sum)
+
+    def taps_of(n):
+        return [short_filt[n, j : j + 1, cols_of(me)] for j in range(taps)]
+
+    gain = gain_in[:, cols_of(me)]
+
+    def at(i, rows=ROWS):
+        return pl.ds(pl.multiple_of(i * rows, rows), rows)
+
+    def short_conv(n, i, weights):
+        piece = branch[n, pl.ds(pl.multiple_of(i * ROWS, ROWS), ROWS + PAD), :].astype(F32)
+        total = weights[0] * piece[PAD : PAD + ROWS]
+        for j in range(1, taps):
+            total = total + weights[j] * piece[PAD - j : PAD - j + ROWS]
+        return total
+
+    def forward(spec):
+        @pl.loop(0, 2 * seq // 256)
+        def _(m):
+            rows = at(m, 256)
+            spec[rows, :] = dot3(wh[rows, :], wl[rows, :], op_h[...], op_l[...])
+
+    def inverse(store):
+        @pl.loop(0, seq // 256)
+        def _(m):
+            rows = at(m, 256)
+            store(rows, dot3(vh[rows, :], vl[rows, :], prod_h[...], prod_l[...]))
+
+    def multiply(left, right, sign):
+        @pl.loop(0, seq // ROWS)
+        def _(i):
+            re = at(i)
+            im = pl.ds(pl.multiple_of(seq + i * ROWS, ROWS), ROWS)
+            a, b = left[re, :], left[im, :] * sign
+            c, d = right[re, :], right[im, :]
+            prod_h[re, :], prod_l[re, :] = halves(a * c - b * d)
+            prod_h[im, :], prod_l[im, :] = halves(a * d + b * c)
+
+    for copy in f_copies:
+        copy.wait_recv()
+    f_own.wait()
+    f_hop = remote(filt.at[dp], filt.at[dp], hop_send, hop_recv, other)
+
+    arrived(1)
+    arrived(2)
+    k_taps = taps_of(1)
+    v_taps = taps_of(2)
+
+    @pl.loop(0, seq // ROWS)
+    def _(i):
+        ks = short_conv(1, i, k_taps)
+        vs = short_conv(2, i, v_taps)
+        shorts[1, at(i), :] = ks
+        shorts[2, at(i), :] = vs
+        op_h[at(i), :], op_l[at(i), :] = halves(ks * vs)
+
+    for copy in tables:
+        copy.wait()
+    forward(spec_kv)
+
+    f_hop.wait_recv()
+
+    @pl.loop(0, seq // ROWS)
+    def _(i):
+        op_h[at(i), :half], op_l[at(i), :half] = halves(filt[0, at(i), :])
+        op_h[at(i), half:], op_l[at(i), half:] = halves(filt[1, at(i), :])
+
+    forward(spec_f)
+    multiply(spec_kv, spec_f, 1.0)
+
+    def store_conv(rows, values):
+        conv[rows, :] = values
+
+    inverse(store_conv)
+
+    arrived(0)
+    arrived(3)
+    q_taps = taps_of(0)
+
+    def folded(values):
+        total = values[:, :128]
+        for n in range(1, width // 128):
+            total = total + values[:, n * 128 : (n + 1) * 128]
+        return total
+
+    @pl.loop(0, seq // ROWS)
+    def _(i):
+        qs = short_conv(0, i, q_taps)
+        shorts[0, at(i), :] = qs
+        y = qs * conv[at(i), :]
+        y_buf[at(i), :] = y
+        gz = branch[3, pl.ds(pl.multiple_of(PAD + i * ROWS, PAD), ROWS), :].astype(F32) * gain
+        sums[0, at(i), :] = folded(y * y)
+        sums[1, at(i), :] = folded(gz * y)
+
+    groups = seq // 128
+    lane = lax.broadcasted_iota(jnp.int32, (128, 128), 1)
+    columns = jnp.zeros((128, 128), F32)
+    for n in range(2):
+        for b in range(groups):
+            part = jnp.sum(sums[n, b * 128 : (b + 1) * 128, :], axis=1, keepdims=True)
+            columns = jnp.where(lane == n * groups + b, part, columns)
+    stats[0] = columns.T[: 2 * groups]
+    st_copies = [
+        remote(
+            stats.at[0],
+            stats.at[a * ctx + b],
+            st_send.at[a * ctx + b],
+            st_recv.at[a * ctx + b],
+            {"tensor": lax.rem(row + a, tens), "context": peer(b)},
+        )
+        for a, b in near
+    ]
+    for copy in st_copies:
+        copy.wait_recv()
+    total = stats[0]
+    for n in range(1, tens * ctx):
+        total = total + stats[n]
+    inv = 1.0 / jnp.sqrt(total[:groups] / model_width + EPS)
+    coef = total[groups:] * (inv * inv * inv / model_width)
+    spread = jnp.concatenate([inv, coef, jnp.zeros((128 - 2 * groups, 128), F32)], 0).T
+
+    for b in range(groups):
+        sums[0, b * 128 : (b + 1) * 128, :] = jnp.broadcast_to(spread[:, b : b + 1], (128, 128))
+        sums[1, b * 128 : (b + 1) * 128, :] = jnp.broadcast_to(
+            spread[:, groups + b : groups + b + 1], (128, 128)
+        )
+
+    def wide(n, i):
+        return jnp.concatenate([sums[n, at(i), :]] * (width // 128), 1)
+
+    @pl.loop(0, seq // ROWS)
+    def _(i):
+        sent[3, at(i), :] = (y_buf[at(i), :] * wide(0, i) * gain).astype(BF16)
+
+    def send_back(n, target):
+        copies = [
+            remote(
+                sent.at[n, rows_of(peer(off)), :],
+                target,
+                out_send.at[n, off],
+                out_recv.at[n, off],
+                {"context": peer(off)},
+            )
+            for off in range(1, ctx)
+        ]
+        return copies, local(sent.at[n, rows_of(me), :], target, out_local.at[n])
+
+    back = [send_back(3, mixed.at[0, :, cols_of(me)])]
+
+    @pl.loop(0, seq // ROWS)
+    def _(i):
+        gz = branch[3, pl.ds(pl.multiple_of(PAD + i * ROWS, PAD), ROWS), :].astype(F32) * gain
+        dy = gz * wide(0, i) - y_buf[at(i), :] * wide(1, i)
+        op_h[at(i), :], op_l[at(i), :] = halves(dy * shorts[0, at(i), :])
+        grads[0, at(i), :] = dy * conv[at(i), :]
+
+    scale = 1.0 / math.sqrt(total_rows)
+
+    def back_short(n):
+        weights = taps_of(n)
+
+        def body(i, acc):
+            piece = grads[n, pl.ds(pl.multiple_of(i * ROWS, ROWS), ROWS + 8), :]
+            total = weights[0] * piece[:ROWS]
+            for j in range(1, taps):
+                total = total + weights[j] * piece[j : j + ROWS]
+            sent[n, at(i), :] = total.astype(BF16)
+            inputs = branch[n, pl.ds(pl.multiple_of(i * ROWS, ROWS), ROWS + PAD), :].astype(F32)
+            own = piece[:ROWS]
+            out = []
+            for j in range(taps):
+                prod = own * inputs[PAD - j : PAD - j + ROWS]
+                part = acc[j]
+                for r in range(ROWS // 8):
+                    part = part + prod[r * 8 : (r + 1) * 8]
+                out.append(part)
+            return tuple(out)
+
+        acc = lax.fori_loop(0, seq // ROWS, body, tuple(jnp.zeros((8, width), F32) for _ in range(taps)))
+        back.append(send_back(n, grad_inputs.at[n, 0, :, cols_of(me)]))
+        for j in range(taps):
+            short_sum[0, n, j : j + 1, :] = jnp.sum(acc[j], axis=0, keepdims=True) * scale
+
+    back_short(0)
+
+    forward(spec_g)
+    multiply(spec_kv, spec_g, -1.0)
+
+    def store_dfilt(rows, values):
+        dfilt[0, rows, :] = values[:, :half] * scale
+        dfilt[1, rows, :] = values[:, half:] * scale
+
+    inverse(store_dfilt)
+    df_copy = remote(dfilt.at[1 - dp], dfilt_in, df_send, df_recv, other)
+
+    multiply(spec_f, spec_g, -1.0)
+
+    def store_dkv(rows, values):
+        grads[1, rows, :] = values * shorts[2, rows, :]
+        grads[2, rows, :] = values * shorts[1, rows, :]
+
+    inverse(store_dkv)
+
+    df_copy.wait_recv()
+    dfilt_sum[...] = dfilt[dp] + dfilt_in[...]
+    gl_target = grad_long.at[:, half_cols(me, dp)]
+    gl_copies = [
+        remote(
+            dfilt_sum.at[rows_of(peer(off)), :],
+            gl_target,
+            gl_send.at[off],
+            gl_recv.at[off],
+            {"context": peer(off)},
+        )
+        for off in range(1, ctx)
+    ]
+    gl_own = local(dfilt_sum.at[rows_of(me), :], gl_target, gl_local)
+    forwards = [remote(dfilt_sum.at[rows_of(me), :], gl_target, fw_send.at[0], fw_recv.at[0], other)]
+
+    back_short(1)
+    back_short(2)
+
+    sh_copy = remote(short_sum.at[0], short_sum.at[1], sh_send, sh_recv, other)
+    for off in range(1, ctx):
+        gl_copies[off - 1].wait_recv()
+        piece = grad_long.at[:, half_cols(source(off), dp)]
+        forwards.append(remote(piece, piece, fw_send.at[off], fw_recv.at[off], other))
+    sh_copy.wait_recv()
+    short_sum[2] = short_sum[0] + short_sum[1]
+    gs_target = grad_short.at[:, :, cols_of(me)]
+    gs_copies = [
+        remote(short_sum.at[2], gs_target, gs_send.at[off], gs_recv.at[off], {"context": peer(off)})
+        for off in range(1, ctx)
+    ]
+    gs_own = local(short_sum.at[2], gs_target, gs_local)
+
+    for copies, own in back:
+        own.wait()
+        for copy in copies:
+            copy.wait()
+    gl_own.wait()
+    for copy in gl_copies:
+        copy.wait_send()
+    for copy in forwards:
+        copy.wait()
+    gs_own.wait()
+    for copy in gs_copies:
+        copy.wait()
+    sh_copy.wait_send()
+    df_copy.wait_send()
+    f_hop.wait_send()
+    for copy in f_copies + st_copies:
+        copy.wait_send()
+    for n in range(4):
+        for copy in arrivals[n][:-1]:
+            copy.wait_send()
+
+
+def fused(q_in, k_in, v_in, short_filt, long_filt, norm_gain, grad_out):
+    _, block, channels = q_in.shape
+    ctx = lax.axis_size("context")
+    tens = lax.axis_size("tensor")
+    seq = block * ctx
+    width = channels // ctx
+    tables = [jnp.asarray(t) for t in odd_tables(seq)]
+    dma = pltpu.SemaphoreType.DMA
+    anywhere = pl.BlockSpec(memory_space=pl.ANY)
+    in_vmem = pl.BlockSpec(memory_space=pltpu.VMEM)
+    outs = pl.pallas_call(
+        functools.partial(operator_kernel, D, lax.axis_size("dp") * seq),
+        out_shape=(
+            jax.ShapeDtypeStruct((1, block, channels), BF16),
+            jax.ShapeDtypeStruct((3, 1, block, channels), BF16),
+            jax.ShapeDtypeStruct((block, channels), F32),
+            jax.ShapeDtypeStruct((3, 8, channels), F32),
+        ),
+        in_specs=[anywhere] * 5 + [in_vmem] * 2 + [anywhere] * 4,
+        out_specs=(anywhere,) * 4,
+        scratch_shapes=[
+            pltpu.VMEM((4, PAD + seq, width), BF16),
+            pltpu.VMEM((2, seq, width // 2), F32),
+            pltpu.VMEM((2 * seq, seq), BF16),
+            pltpu.VMEM((2 * seq, seq), BF16),
+            pltpu.VMEM((seq, 2 * seq), BF16),
+            pltpu.VMEM((seq, 2 * seq), BF16),
+            pltpu.VMEM((3, seq, width), F32),
+            pltpu.VMEM((seq, width), BF16),
+            pltpu.VMEM((seq, width), BF16),
+            pltpu.VMEM((2 * seq, width), F32),
+            pltpu.VMEM((2 * seq, width), F32),
+            pltpu.VMEM((2 * seq, width), F32),
+            pltpu.VMEM((2 * seq, width), BF16),
+            pltpu.VMEM((2 * seq, width), BF16),
+            pltpu.VMEM((seq, width), F32),
+            pltpu.VMEM((seq, width), F32),
+            pltpu.VMEM((2, seq, 128), F32),
+            pltpu.VMEM((tens * ctx, 2 * seq // 128, 128), F32),
+            pltpu.VMEM((3, seq + 8, width), F32),
+            pltpu.VMEM((2, seq, width // 2), F32),
+            pltpu.VMEM((seq, width // 2), F32),
+            pltpu.VMEM((seq, width // 2), F32),
+            pltpu.VMEM((3, 3, 8, width), F32),
+            pltpu.VMEM((4, seq, width), BF16),
+            dma((5, ctx)),
+            dma((5, ctx)),
+            dma((5,)),
+            dma,
+            dma,
+            dma((4,)),
+            dma((tens * ctx,)),
+            dma((tens * ctx,)),
+            dma((4, ctx)),
+            dma((4, ctx)),
+            dma((4,)),
+            dma,
+            dma,
+            dma((ctx,)),
+            dma((ctx,)),
+            dma,
+            dma((ctx,)),
+            dma((ctx,)),
+            dma,
+            dma,
+            dma((ctx,)),
+            dma((ctx,)),
+            dma,
+        ],
+        compiler_params=pltpu.CompilerParams(
+            collective_id=0, has_side_effects=True, vmem_limit_bytes=48 * 2**20
+        ),
+    )(
+        q_in[0],
+        k_in[0],
+        v_in[0],
+        grad_out[0],
+        long_filt,
+        short_filt,
+        norm_gain[None],
+        *tables,
+    )
+    mixed, grad_inputs, grad_long, short = outs
+    return mixed, grad_inputs, grad_long, short[:, : short_filt.shape[1]]
+
+
+def operator(q_in, k_in, v_in, short_filt, long_filt, norm_gain, grad_out):
+    _, block, channels = q_in.shape
+    ctx = lax.axis_size("context")
+    dense = block * ctx <= 1024 and block % 128 == 0 and channels % (256 * ctx) == 0
+    form = fused if dense and lax.axis_size("dp") == 2 else shards
+    return form(q_in, k_in, v_in, short_filt, long_filt, norm_gain, grad_out)
+
 
 def solution(mesh):
     in_specs = (
@@ -171,4 +716,4 @@
         P("context", "tensor"),
         P(None, None, "tensor"),
     )
-    return jax.shard_map(shards, mesh=mesh, in_specs=in_specs, out_specs=out_specs, check_vma=False)
+    return jax.shard_map(operator, mesh=mesh, in_specs=in_specs, out_specs=out_specs, check_vma=False)

time: 634 us -> 88.6 us (0.14); the launches traced: 625 us -> 88.2 us
  waiting for transfers between devices: 267 us -> 0 us
  blocking collectives: 197 us -> 0 us
  Pallas kernels: 0 us -> 75.7 us
  local copies, waits for them, and re-layouts: 66.6 us -> 11.9 us
  matrix products: 35 us -> 0 us
  starting transfers between devices: 25.7 us -> 0 us
  other arithmetic: 18.7 us -> 0 us
  between operations: 15.2 us -> 0.66 us
    all_to_all x4 -> x0, blocking collectives: 190 us -> none  [the longest x1 96.2 us: inverse_rows(): lax.all_to_all(turned, 'context', split_axis=3, concat_axis=2, tiled=True)]
    all_to_all x4 -> x0, waiting for transfers between devices: 174 us -> none  [the longest x1 89.8 us: forward_rows(): lax.all_to_all(turned, 'context', split_axis=2, concat_axis=3, tiled=True)]
    psum x2 -> x0, waiting for transfers between devices: 86.8 us -> none  [the longest x1 57.6 us: shards(): grad_short = lax.psum(short_local, ('dp', 'context')) * scale]
    pallas_call x0 -> x1, Pallas kernels: none -> 75.7 us  [fused(): pl.pallas_call(functools.partial(operator_kernel, D, lax.axis_size('dp')...]
    dot_general x8 -> x0, matrix products: 35 us -> none  [the longest x2 10.7 us: forward_rows(): jnp.einsum('pqmb,nqjbx->npjmx', block_table(block_len, 1.0), moved, preci...]
    all_to_all x9 -> x0, local copies, waits for them, and re-layouts: 25.7 us -> none  [the longest x5 19.6 us: inverse_rows(): lax.all_to_all(turned, 'context', split_axis=3, concat_axis=2, tiled=True)]
    all_to_all x4 -> x0, starting transfers between devices: 19.3 us -> none  [the longest x2 9.77 us: forward_rows(): lax.all_to_all(values.reshape(count, 1, block_len, width), 'context', spl...]
    transpose x4 -> x0, local copies, waits for them, and re-layouts: 18.4 us -> none  [the longest x2 11.6 us: inverse_rows(): turned = jnp.einsum('pqjmb,nqjmx->npjbx', table, spec, precision=HIGH)]
  transfers between devices with their start and end apart: 8 -> 0, of which waited for: 8 -> 0; matrix products, arithmetic and copies ran while one was open for 2% -> 0% of each run, Pallas kernels for 0% -> 0%
where the time goes in v1:
time: 88.6 us; the launch traced here: 88.2 us
  Pallas kernels  75.7 us (85%)
  local copies, waits for them, and re-layouts  11.9 us (13%)
    pallas_call x1, Pallas kernels, fused(): pl.pallas_call(functools.partial(operator_kernel, D, lax.axis_size('dp')...  75.7 us
    unnamed x22, local copies, waits for them, and re-layouts  11.9 us

profile of v1, /device:TPU:0, one launch (start us, length us, event | category | flops | bytes accessed | tf_op | source)
XLA Modules:
  0.0 88.2 jit_solution(1981780146352440639)
XLA Ops:
  0.6 0.0 copy-start.8
  0.6 0.7 copy-done.8
  1.3 0.0 copy-start
  1.3 1.2 %copy-done = bf16[1024,512]{1,0:T(8,128)(2,1)S(1)} copy-done((bf16[1024,512]{1,0:T(8,128)(2,1)S(1)}, bf16[1024,512]{1,0:T(8,128)(2,1)}, u32[]{:S(2)}) %copy-start) | copy-done | bytes 1048600
  2.5 0.0 copy-start.1
  2.5 1.2 %copy-done.1 = bf16[1024,512]{1,0:T(8,128)(2,1)S(1)} copy-done((bf16[1024,512]{1,0:T(8,128)(2,1)S(1)}, bf16[1024,512]{1,0:T(8,128)(2,1)}, u32[]{:S(2)}) %copy-start.1) | copy-done | bytes 1048600
  3.8 0.0 copy-start.2
  3.8 1.0 %copy-done.2 = f32[128,1024]{1,0:T(8,128)S(1)} copy-done((f32[128,1024]{1,0:T(8,128)S(1)}, f32[128,1024]{1,0:T(8,128)}, u32[]{:S(2)}) %copy-start.2) | copy-done | bytes 524312
  4.8 0.0 copy-start.3
  4.8 0.9 %copy-done.3 = bf16[1,128,1024]{2,1,0:T(8,128)(2,1)S(1)} copy-done((bf16[1,128,1024]{2,1,0:T(8,128)(2,1)S(1)}, bf16[1,128,1024]{2,1,0:T(8,128)(2,1)}, u32[]{:S(2)}) %copy-start.3) | copy-done | bytes 262168
  5.8 0.0 copy-start.4
  5.8 0.9 %copy-done.4 = bf16[1,128,1024]{2,1,0:T(8,128)(2,1)S(1)} copy-done((bf16[1,128,1024]{2,1,0:T(8,128)(2,1)S(1)}, bf16[1,128,1024]{2,1,0:T(8,128)(2,1)}, u32[]{:S(2)}) %copy-start.4) | copy-done | bytes 262168
  6.7 0.0 copy-start.5
  6.7 0.9 %copy-done.5 = bf16[1,128,1024]{2,1,0:T(8,128)(2,1)S(1)} copy-done((bf16[1,128,1024]{2,1,0:T(8,128)(2,1)S(1)}, bf16[1,128,1024]{2,1,0:T(8,128)(2,1)}, u32[]{:S(2)}) %copy-start.5) | copy-done | bytes 262168
  7.7 0.0 copy-start.6
  7.7 0.9 %copy-done.6 = bf16[1,128,1024]{2,1,0:T(8,128)(2,1)S(1)} copy-done((bf16[1,128,1024]{2,1,0:T(8,128)(2,1)S(1)}, bf16[1,128,1024]{2,1,0:T(8,128)(2,1)}, u32[]{:S(2)}) %copy-start.6) | copy-done | bytes 262168
  8.6 0.0 copy-start.7
  8.6 0.9 %copy-done.7 = f32[3,7,1024]{2,1,0:T(8,128)S(1)} copy-done((f32[3,7,1024]{2,1,0:T(8,128)S(1)}, f32[3,7,1024]{2,1,0:T(8,128)}, u32[]{:S(2)}) %copy-start.7) | copy-done | bytes 86040
  9.5 75.7 %shard_map.138 = (bf16[1,128,1024]{2,1,0:T(8,128)(2,1)S(1)}, bf16[3,1,128,1024]{3,2,1,0:T(8,128)(2,1)S(1)}, f32[128,1024]{1,0:T(8,128)S(1)}, f32[3,8,1024]{2,1,0:T(8,128)S(1)}) custom-call(bf16[128,1024]{1,0:T(8,128)(2,1)S(1)} %bitcast.6, bf16[128,1024]{1,0:T(8,128)(2,1)S(1)} %bitcast.7, bf16[128,1024]{1,0:T(8,128)(2,1)S(1)} %bitcast.8, ...), custom_call_target="tpu_custom_call" | custom-call | tf_op jit(solution)/shard_map/pallas_call | solution.py:619
  85.2 0.7 copy.19
  85.9 0.9 copy.20
  86.8 0.8 copy.21
  87.6 0.6 copy.22
Async XLA Ops:
  0.6 0.7 copy-start.8
  1.3 1.2 %copy-start = (bf16[1024,512]{1,0:T(8,128)(2,1)S(1)}, bf16[1024,512]{1,0:T(8,128)(2,1)}, u32[]{:S(2)}) copy-start(bf16[1024,512]{1,0:T(8,128)(2,1)} %constant.9.clone.wl_in) | copy-start | bytes 3145732
  2.5 1.2 %copy-start.1 = (bf16[1024,512]{1,0:T(8,128)(2,1)S(1)}, bf16[1024,512]{1,0:T(8,128)(2,1)}, u32[]{:S(2)}) copy-start(bf16[1024,512]{1,0:T(8,128)(2,1)} %constant.8.clone.wh_in) | copy-start | bytes 3145732
  3.8 1.0 %copy-start.2 = (f32[128,1024]{1,0:T(8,128)S(1)}, f32[128,1024]{1,0:T(8,128)}, u32[]{:S(2)}) copy-start(f32[128,1024]{1,0:T(8,128)} %f_in.1) | copy-start | bytes 1572868
  4.8 0.9 %copy-start.3 = (bf16[1,128,1024]{2,1,0:T(8,128)(2,1)S(1)}, bf16[1,128,1024]{2,1,0:T(8,128)(2,1)}, u32[]{:S(2)}) copy-start(bf16[1,128,1024]{2,1,0:T(8,128)(2,1)} %param.11) | copy-start | bytes 786436
  5.8 0.9 %copy-start.4 = (bf16[1,128,1024]{2,1,0:T(8,128)(2,1)S(1)}, bf16[1,128,1024]{2,1,0:T(8,128)(2,1)}, u32[]{:S(2)}) copy-start(bf16[1,128,1024]{2,1,0:T(8,128)(2,1)} %param.12) | copy-start | bytes 786436
  6.7 0.9 %copy-start.5 = (bf16[1,128,1024]{2,1,0:T(8,128)(2,1)S(1)}, bf16[1,128,1024]{2,1,0:T(8,128)(2,1)}, u32[]{:S(2)}) copy-start(bf16[1,128,1024]{2,1,0:T(8,128)(2,1)} %param.13) | copy-start | bytes 786436
  7.7 0.9 %copy-start.6 = (bf16[1,128,1024]{2,1,0:T(8,128)(2,1)S(1)}, bf16[1,128,1024]{2,1,0:T(8,128)(2,1)}, u32[]{:S(2)}) copy-start(bf16[1,128,1024]{2,1,0:T(8,128)(2,1)} %param.17) | copy-start | bytes 786436
  8.6 0.9 %copy-start.7 = (f32[3,7,1024]{2,1,0:T(8,128)S(1)}, f32[3,7,1024]{2,1,0:T(8,128)}, u32[]{:S(2)}) copy-start(f32[3,7,1024]{2,1,0:T(8,128)} %short_filt.1) | copy-start | bytes 258052

commit v2 on v1

--- a/solution.py
+++ b/solution.py
@@ -199,8 +199,8 @@
     v_in,
     g_in,
     f_in,
-    short_filt,
-    gain_in,
+    short_in,
+    gains_in,
     wh_in,
     wl_in,
     vh_in,
@@ -215,6 +215,8 @@
     wl,
     vh,
     vl,
+    short_filt,
+    gain_in,
     shorts,
     op_h,
     op_l,
@@ -296,11 +298,6 @@
         copy.start()
         return copy
 
-    tables = [
-        local(src, dst, tab_sem.at[n])
-        for n, (src, dst) in enumerate([(wh_in, wh), (wl_in, wl), (vh_in, vh), (vl_in, vl)])
-    ]
-
     barrier = pltpu.get_barrier_semaphore()
     near = [(a, b) for a in range(tens) for b in range(ctx) if a + b > 0]
     for a, b in near:
@@ -339,6 +336,12 @@
         ]
         arrivals[n].append(local(ref.at[:, cols_of(me)], branch.at[n, land, :], in_local.at[n]))
 
+    small = [local(short_in, short_filt, tab_sem.at[4]), local(gains_in, gain_in, tab_sem.at[5])]
+    tables = [
+        local(src, dst, tab_sem.at[n])
+        for n, (src, dst) in enumerate([(wh_in, wh), (wl_in, wl), (vh_in, vh), (vl_in, vl)])
+    ]
+
     def arrived(n):
         for copy in arrivals[n][:-1]:
             copy.wait_recv()
@@ -347,6 +350,9 @@
     branch[:, :PAD, :] = jnp.zeros((4, PAD, width), BF16)
     grads[:, seq:, :] = jnp.zeros((3, 8, width), F32)
     short_sum[...] = jnp.zeros_like(short_sum)
+
+    for copy in small:
+        copy.wait()
 
     def taps_of(n):
         return [short_filt[n, j : j + 1, cols_of(me)] for j in range(taps)]
@@ -391,22 +397,14 @@
     f_hop = remote(filt.at[dp], filt.at[dp], hop_send, hop_recv, other)
 
     arrived(1)
-    arrived(2)
     k_taps = taps_of(1)
-    v_taps = taps_of(2)
 
     @pl.loop(0, seq // ROWS)
     def _(i):
-        ks = short_conv(1, i, k_taps)
-        vs = short_conv(2, i, v_taps)
-        shorts[1, at(i), :] = ks
-        shorts[2, at(i), :] = vs
-        op_h[at(i), :], op_l[at(i), :] = halves(ks * vs)
+        shorts[1, at(i), :] = short_conv(1, i, k_taps)
 
     for copy in tables:
         copy.wait()
-    forward(spec_kv)
-
     f_hop.wait_recv()
 
     @pl.loop(0, seq // ROWS)
@@ -415,6 +413,17 @@
         op_h[at(i), half:], op_l[at(i), half:] = halves(filt[1, at(i), :])
 
     forward(spec_f)
+
+    arrived(2)
+    v_taps = taps_of(2)
+
+    @pl.loop(0, seq // ROWS)
+    def _(i):
+        vs = short_conv(2, i, v_taps)
+        shorts[2, at(i), :] = vs
+        op_h[at(i), :], op_l[at(i), :] = halves(shorts[1, at(i), :] * vs)
+
+    forward(spec_kv)
     multiply(spec_kv, spec_f, 1.0)
 
     def store_conv(rows, values):
@@ -423,7 +432,6 @@
     inverse(store_conv)
 
     arrived(0)
-    arrived(3)
     q_taps = taps_of(0)
 
     def folded(values):
@@ -438,42 +446,52 @@
         shorts[0, at(i), :] = qs
         y = qs * conv[at(i), :]
         y_buf[at(i), :] = y
-        gz = branch[3, pl.ds(pl.multiple_of(PAD + i * ROWS, PAD), ROWS), :].astype(F32) * gain
         sums[0, at(i), :] = folded(y * y)
-        sums[1, at(i), :] = folded(gz * y)
 
     groups = seq // 128
     lane = lax.broadcasted_iota(jnp.int32, (128, 128), 1)
-    columns = jnp.zeros((128, 128), F32)
-    for n in range(2):
+
+    def share(n):
+        columns = jnp.zeros((128, 128), F32)
         for b in range(groups):
             part = jnp.sum(sums[n, b * 128 : (b + 1) * 128, :], axis=1, keepdims=True)
-            columns = jnp.where(lane == n * groups + b, part, columns)
-    stats[0] = columns.T[: 2 * groups]
-    st_copies = [
-        remote(
-            stats.at[0],
-            stats.at[a * ctx + b],
-            st_send.at[a * ctx + b],
-            st_recv.at[a * ctx + b],
-            {"tensor": lax.rem(row + a, tens), "context": peer(b)},
-        )
-        for a, b in near
-    ]
-    for copy in st_copies:
-        copy.wait_recv()
-    total = stats[0]
-    for n in range(1, tens * ctx):
-        total = total + stats[n]
-    inv = 1.0 / jnp.sqrt(total[:groups] / model_width + EPS)
-    coef = total[groups:] * (inv * inv * inv / model_width)
-    spread = jnp.concatenate([inv, coef, jnp.zeros((128 - 2 * groups, 128), F32)], 0).T
-
-    for b in range(groups):
-        sums[0, b * 128 : (b + 1) * 128, :] = jnp.broadcast_to(spread[:, b : b + 1], (128, 128))
-        sums[1, b * 128 : (b + 1) * 128, :] = jnp.broadcast_to(
-            spread[:, groups + b : groups + b + 1], (128, 128)
-        )
+            columns = jnp.where(lane == b, part, columns)
+        stats[n, 0] = columns.T[:8]
+        return [
+            remote(
+                stats.at[n, 0],
+                stats.at[n, a * ctx + b],
+                st_send.at[n, a * ctx + b],
+                st_recv.at[n, a * ctx + b],
+                {"tensor": lax.rem(row + a, tens), "context": peer(b)},
+            )
+            for a, b in near
+        ]
+
+    def gathered(n, copies):
+        for copy in copies:
+            copy.wait_recv()
+        total = stats[n, 0]
+        for r in range(1, tens * ctx):
+            total = total + stats[n, r]
+        return total
+
+    def widen(n, values):
+        spread = jnp.concatenate([values, jnp.zeros((120, 128), F32)], 0).T
+        for b in range(groups):
+            sums[n, b * 128 : (b + 1) * 128, :] = jnp.broadcast_to(spread[:, b : b + 1], (128, 128))
+
+    st_copies = share(0)
+    arrived(3)
+
+    @pl.loop(0, seq // ROWS)
+    def _(i):
+        gz = branch[3, pl.ds(pl.multiple_of(PAD + i * ROWS, PAD), ROWS), :].astype(F32) * gain
+        sums[1, at(i), :] = folded(gz * y_buf[at(i), :])
+
+    prod_copies = share(1)
+    inv = 1.0 / jnp.sqrt(gathered(0, st_copies) / model_width + EPS)
+    widen(0, inv)
 
     def wide(n, i):
         return jnp.concatenate([sums[n, at(i), :]] * (width // 128), 1)
@@ -496,6 +514,7 @@
         return copies, local(sent.at[n, rows_of(me), :], target, out_local.at[n])
 
     back = [send_back(3, mixed.at[0, :, cols_of(me)])]
+    widen(1, gathered(1, prod_copies) * (inv * inv * inv / model_width))
 
     @pl.loop(0, seq // ROWS)
     def _(i):
@@ -509,14 +528,20 @@
     def back_short(n):
         weights = taps_of(n)
 
-        def body(i, acc):
+        @pl.loop(0, seq // ROWS)
+        def _(i):
             piece = grads[n, pl.ds(pl.multiple_of(i * ROWS, ROWS), ROWS + 8), :]
             total = weights[0] * piece[:ROWS]
             for j in range(1, taps):
                 total = total + weights[j] * piece[j : j + ROWS]
             sent[n, at(i), :] = total.astype(BF16)
+
+        back.append(send_back(n, grad_inputs.at[n, 0, :, cols_of(me)]))
+
+    def short_grads(n):
+        def body(i, acc):
+            own = grads[n, at(i), :]
             inputs = branch[n, pl.ds(pl.multiple_of(i * ROWS, ROWS), ROWS + PAD), :].astype(F32)
-            own = piece[:ROWS]
             out = []
             for j in range(taps):
                 prod = own * inputs[PAD - j : PAD - j + ROWS]
@@ -527,13 +552,22 @@
             return tuple(out)
 
         acc = lax.fori_loop(0, seq // ROWS, body, tuple(jnp.zeros((8, width), F32) for _ in range(taps)))
-        back.append(send_back(n, grad_inputs.at[n, 0, :, cols_of(me)]))
         for j in range(taps):
             short_sum[0, n, j : j + 1, :] = jnp.sum(acc[j], axis=0, keepdims=True) * scale
 
     back_short(0)
 
     forward(spec_g)
+    multiply(spec_f, spec_g, -1.0)
+
+    def store_dkv(rows, values):
+        grads[1, rows, :] = values * shorts[2, rows, :]
+        grads[2, rows, :] = values * shorts[1, rows, :]
+
+    inverse(store_dkv)
+    back_short(1)
+    back_short(2)
+
     multiply(spec_kv, spec_g, -1.0)
 
     def store_dfilt(rows, values):
@@ -543,13 +577,9 @@
     inverse(store_dfilt)
     df_copy = remote(dfilt.at[1 - dp], dfilt_in, df_send, df_recv, other)
 
-    multiply(spec_f, spec_g, -1.0)
-
-    def store_dkv(rows, values):
-        grads[1, rows, :] = values * shorts[2, rows, :]
-        grads[2, rows, :] = values * shorts[1, rows, :]
-
-    inverse(store_dkv)
+    for n in range(3):
+        short_grads(n)
+    sh_copy = remote(short_sum.at[0], short_sum.at[1], sh_send, sh_recv, other)
 
     df_copy.wait_recv()
     dfilt_sum[...] = dfilt[dp] + dfilt_in[...]
@@ -567,14 +597,6 @@
     gl_own = local(dfilt_sum.at[rows_of(me), :], gl_target, gl_local)
     forwards = [remote(dfilt_sum.at[rows_of(me), :], gl_target, fw_send.at[0], fw_recv.at[0], other)]
 
-    back_short(1)
-    back_short(2)
-
-    sh_copy = remote(short_sum.at[0], short_sum.at[1], sh_send, sh_recv, other)
-    for off in range(1, ctx):
-        gl_copies[off - 1].wait_recv()
-        piece = grad_long.at[:, half_cols(source(off), dp)]
-        forwards.append(remote(piece, piece, fw_send.at[off], fw_recv.at[off], other))
     sh_copy.wait_recv()
     short_sum[2] = short_sum[0] + short_sum[1]
     gs_target = grad_short.at[:, :, cols_of(me)]
@@ -583,6 +605,10 @@
         for off in range(1, ctx)
     ]
     gs_own = local(short_sum.at[2], gs_target, gs_local)
+    for off in range(1, ctx):
+        gl_copies[off - 1].wait_recv()
+        piece = grad_long.at[:, half_cols(source(off), dp)]
+        forwards.append(remote(piece, piece, fw_send.at[off], fw_recv.at[off], other))
 
     for copies, own in back:
         own.wait()
@@ -599,7 +625,7 @@
     sh_copy.wait_send()
     df_copy.wait_send()
     f_hop.wait_send()
-    for copy in f_copies + st_copies:
+    for copy in f_copies + st_copies + prod_copies:
         copy.wait_send()
     for n in range(4):
         for copy in arrivals[n][:-1]:
@@ -615,7 +641,7 @@
     tables = [jnp.asarray(t) for t in odd_tables(seq)]
     dma = pltpu.SemaphoreType.DMA
     anywhere = pl.BlockSpec(memory_space=pl.ANY)
-    in_vmem = pl.BlockSpec(memory_space=pltpu.VMEM)
+    in_hbm = pl.BlockSpec(memory_space=pltpu.HBM)
     outs = pl.pallas_call(
         functools.partial(operator_kernel, D, lax.axis_size("dp") * seq),
         out_shape=(
@@ -624,7 +650,7 @@
             jax.ShapeDtypeStruct((block, channels), F32),
             jax.ShapeDtypeStruct((3, 8, channels), F32),
         ),
-        in_specs=[anywhere] * 5 + [in_vmem] * 2 + [anywhere] * 4,
+        in_specs=[in_hbm] * 11,
         out_specs=(anywhere,) * 4,
         scratch_shapes=[
             pltpu.VMEM((4, PAD + seq, width), BF16),
@@ -633,6 +659,8 @@
             pltpu.VMEM((2 * seq, seq), BF16),
             pltpu.VMEM((seq, 2 * seq), BF16),
             pltpu.VMEM((seq, 2 * seq), BF16),
+            pltpu.VMEM(short_filt.shape, F32),
+            pltpu.VMEM((1, channels), F32),
             pltpu.VMEM((3, seq, width), F32),
             pltpu.VMEM((seq, width), BF16),
             pltpu.VMEM((seq, width), BF16),
@@ -644,7 +672,7 @@
             pltpu.VMEM((seq, width), F32),
             pltpu.VMEM((seq, width), F32),
             pltpu.VMEM((2, seq, 128), F32),
-            pltpu.VMEM((tens * ctx, 2 * seq // 128, 128), F32),
+            pltpu.VMEM((2, tens * ctx, 8, 128), F32),
             pltpu.VMEM((3, seq + 8, width), F32),
             pltpu.VMEM((2, seq, width // 2), F32),
             pltpu.VMEM((seq, width // 2), F32),
@@ -656,9 +684,9 @@
             dma((5,)),
             dma,
             dma,
-            dma((4,)),
-            dma((tens * ctx,)),
-            dma((tens * ctx,)),
+            dma((6,)),
+            dma((2, tens * ctx)),
+            dma((2, tens * ctx)),
             dma((4, ctx)),
             dma((4, ctx)),
             dma((4,)),
@@ -676,7 +704,7 @@
             dma,
         ],
         compiler_params=pltpu.CompilerParams(
-            collective_id=0, has_side_effects=True, vmem_limit_bytes=48 * 2**20
+            collective_id=0, has_side_effects=True, vmem_limit_bytes=60 * 2**20
         ),
     )(
         q_in[0],

time: 88.6 us -> 83.1 us (0.938)
  local copies, waits for them, and re-layouts: 11.9 us -> 5.4 us
  Pallas kernels: 75.7 us -> 76.9 us
    unnamed x22 -> x8, local copies, waits for them, and re-layouts: 11.9 us -> 5.4 us
    pallas_call x1, Pallas kernels: 75.7 us -> 76.9 us  [fused(): pl.pallas_call(functools.partial(operator_kernel, D, lax.axis_size('dp')...]
where the time goes in v2:
time: 83.1 us; the launch traced here: 82.9 us
  Pallas kernels  76.9 us (93%)
  local copies, waits for them, and re-layouts  5.4 us (6%)
    pallas_call x1, Pallas kernels, fused(): pl.pallas_call(functools.partial(operator_kernel, D, lax.axis_size('dp')...  76.9 us
    unnamed x8, local copies, waits for them, and re-layouts  5.4 us

profile of v2, /device:TPU:0, one launch (start us, length us, event | category | flops | bytes accessed | tf_op | source)
XLA Modules:
  0.0 82.9 jit_solution(9495932532147573044)
XLA Ops:
  0.6 76.9 %shard_map.138 = (bf16[1,128,1024]{2,1,0:T(8,128)(2,1)}, bf16[3,1,128,1024]{3,2,1,0:T(8,128)(2,1)}, f32[128,1024]{1,0:T(8,128)}, f32[3,8,1024]{2,1,0:T(8,128)}) custom-call(bf16[128,1024]{1,0:T(8,128)(2,1)} %bitcast.6, bf16[128,1024]{1,0:T(8,128)(2,1)} %bitcast.7, bf16[128,1024]{1,0:T(8,128)(2,1)} %bitcast.8, bf16[128,1024]{1,0:T(8,128)(2,1)} %bitcast.9, ...), custom_call_target="tpu_custom_call" | custom-call | tf_op jit(solution)/shard_map/pallas_call | solution.py:645
  77.5 1.7 %copy.19 = bf16[1,128,1024]{2,1,0:T(8,128)(2,1)} copy(bf16[1,128,1024]{2,1,0:T(8,128)(2,1)} %get-tuple-element.16) | data formatting | bytes 524288
  79.2 0.0 copy-start
  79.2 2.1 %copy.20 = bf16[3,1,128,1024]{3,2,1,0:T(8,128)(2,1)} copy(bf16[3,1,128,1024]{3,2,1,0:T(8,128)(2,1)} %get-tuple-element.17) | data formatting | bytes 1572864
  81.3 0.0 copy-done
  81.3 0.0 copy-start.1
  81.3 0.8 copy.21
  82.1 0.2 copy-done.1
  82.3 0.6 copy.22
Async XLA Ops:
  79.2 2.1 %copy-start = (f32[128,1024]{1,0:T(8,128)S(1)}, f32[128,1024]{1,0:T(8,128)}, u32[]{:S(2)}) copy-start(f32[128,1024]{1,0:T(8,128)} %get-tuple-element.18) | copy-start | bytes 1572868
  81.3 1.0 %copy-start.1 = (f32[3,8,1024]{2,1,0:T(8,128)S(1)}, f32[3,8,1024]{2,1,0:T(8,128)}, u32[]{:S(2)}) copy-start(f32[3,8,1024]{2,1,0:T(8,128)} %get-tuple-element.11) | copy-start | bytes 294916

commit v3 on v2

--- a/solution.py
+++ b/solution.py
@@ -323,7 +323,10 @@
     f_own = local(f_in.at[:, half_cols(me, dp)], filt.at[dp, rows_of(me), :], in_local.at[4])
     land = pl.ds(pl.multiple_of(PAD + me * block, PAD), block)
     arrivals = {}
-    for n, ref in ((1, k_in), (2, v_in), (0, q_in), (3, g_in)):
+    branch_refs = (q_in, k_in, v_in, g_in)
+
+    def fetch(n):
+        ref = branch_refs[n]
         arrivals[n] = [
             remote(
                 ref.at[:, cols_of(peer(off))],
@@ -336,6 +339,7 @@
         ]
         arrivals[n].append(local(ref.at[:, cols_of(me)], branch.at[n, land, :], in_local.at[n]))
 
+    fetch(1)
     small = [local(short_in, short_filt, tab_sem.at[4]), local(gains_in, gain_in, tab_sem.at[5])]
     tables = [
         local(src, dst, tab_sem.at[n])
@@ -349,7 +353,6 @@
 
     branch[:, :PAD, :] = jnp.zeros((4, PAD, width), BF16)
     grads[:, seq:, :] = jnp.zeros((3, 8, width), F32)
-    short_sum[...] = jnp.zeros_like(short_sum)
 
     for copy in small:
         copy.wait()
@@ -395,8 +398,10 @@
         copy.wait_recv()
     f_own.wait()
     f_hop = remote(filt.at[dp], filt.at[dp], hop_send, hop_recv, other)
+    fetch(2)
 
     arrived(1)
+    fetch(0)
     k_taps = taps_of(1)
 
     @pl.loop(0, seq // ROWS)
@@ -415,6 +420,7 @@
     forward(spec_f)
 
     arrived(2)
+    fetch(3)
     v_taps = taps_of(2)
 
     @pl.loop(0, seq // ROWS)
@@ -558,6 +564,15 @@
     back_short(0)
 
     forward(spec_g)
+    multiply(spec_kv, spec_g, -1.0)
+
+    def store_dfilt(rows, values):
+        dfilt[0, rows, :] = values[:, :half] * scale
+        dfilt[1, rows, :] = values[:, half:] * scale
+
+    inverse(store_dfilt)
+    df_copy = remote(dfilt.at[1 - dp], dfilt_in, df_send, df_recv, other)
+
     multiply(spec_f, spec_g, -1.0)
 
     def store_dkv(rows, values):
@@ -566,23 +581,8 @@
 
     inverse(store_dkv)
     back_short(1)
-    back_short(2)
-
-    multiply(spec_kv, spec_g, -1.0)
-
-    def store_dfilt(rows, values):
-        dfilt[0, rows, :] = values[:, :half] * scale
-        dfilt[1, rows, :] = values[:, half:] * scale
-
-    inverse(store_dfilt)
-    df_copy = remote(dfilt.at[1 - dp], dfilt_in, df_send, df_recv, other)
-
-    for n in range(3):
-        short_grads(n)
-    sh_copy = remote(short_sum.at[0], short_sum.at[1], sh_send, sh_recv, other)
-
     df_copy.wait_recv()
-    dfilt_sum[...] = dfilt[dp] + dfilt_in[...]
+    dfilt_sum[...] = (dfilt[dp] + dfilt_in[...]).astype(BF16)
     gl_target = grad_long.at[:, half_cols(me, dp)]
     gl_copies = [
         remote(
@@ -597,6 +597,16 @@
     gl_own = local(dfilt_sum.at[rows_of(me), :], gl_target, gl_local)
     forwards = [remote(dfilt_sum.at[rows_of(me), :], gl_target, fw_send.at[0], fw_recv.at[0], other)]
 
+    back_short(2)
+
+    for n in range(3):
+        short_grads(n)
+    sh_copy = remote(short_sum.at[0], short_sum.at[1], sh_send, sh_recv, other)
+
+    for off in range(1, ctx):
+        gl_copies[off - 1].wait_recv()
+        piece = grad_long.at[:, half_cols(source(off), dp)]
+        forwards.append(remote(piece, piece, fw_send.at[off], fw_recv.at[off], other))
     sh_copy.wait_recv()
     short_sum[2] = short_sum[0] + short_sum[1]
     gs_target = grad_short.at[:, :, cols_of(me)]
@@ -605,11 +615,6 @@
         for off in range(1, ctx)
     ]
     gs_own = local(short_sum.at[2], gs_target, gs_local)
-    for off in range(1, ctx):
-        gl_copies[off - 1].wait_recv()
-        piece = grad_long.at[:, half_cols(source(off), dp)]
-        forwards.append(remote(piece, piece, fw_send.at[off], fw_recv.at[off], other))
-
     for copies, own in back:
         own.wait()
         for copy in copies:
@@ -632,6 +637,28 @@
             copy.wait_send()
 
 
+def deliver_kernel(
+    mixed, grad_inputs, grad_long, grad_short, mixed_out, inputs_out, long_out, short_out, narrow, wide, sem
+):
+    load = pltpu.make_async_copy(grad_long, narrow, sem.at[0])
+    load.start()
+    copies = [
+        pltpu.make_async_copy(mixed, mixed_out, sem.at[1]),
+        pltpu.make_async_copy(grad_short, short_out, sem.at[2]),
+    ]
+    for n in range(3):
+        copies.append(pltpu.make_async_copy(grad_inputs.at[n], inputs_out.at[n], sem.at[3 + n]))
+    for copy in copies:
+        copy.start()
+    load.wait()
+    wide[...] = narrow[...].astype(F32)
+    store = pltpu.make_async_copy(wide, long_out, sem.at[6])
+    store.start()
+    store.wait()
+    for copy in copies:
+        copy.wait()
+
+
 def fused(q_in, k_in, v_in, short_filt, long_filt, norm_gain, grad_out):
     _, block, channels = q_in.shape
     ctx = lax.axis_size("context")
@@ -647,8 +674,8 @@
         out_shape=(
             jax.ShapeDtypeStruct((1, block, channels), BF16),
             jax.ShapeDtypeStruct((3, 1, block, channels), BF16),
-            jax.ShapeDtypeStruct((block, channels), F32),
-            jax.ShapeDtypeStruct((3, 8, channels), F32),
+            jax.ShapeDtypeStruct((block, channels), BF16),
+            jax.ShapeDtypeStruct(short_filt.shape, F32),
         ),
         in_specs=[in_hbm] * 11,
         out_specs=(anywhere,) * 4,
@@ -676,8 +703,8 @@
             pltpu.VMEM((3, seq + 8, width), F32),
             pltpu.VMEM((2, seq, width // 2), F32),
             pltpu.VMEM((seq, width // 2), F32),
-            pltpu.VMEM((seq, width // 2), F32),
-            pltpu.VMEM((3, 3, 8, width), F32),
+            pltpu.VMEM((seq, width // 2), BF16),
+            pltpu.VMEM((3, 3, short_filt.shape[1], width), F32),
             pltpu.VMEM((4, seq, width), BF16),
             dma((5, ctx)),
             dma((5, ctx)),
@@ -716,8 +743,23 @@
         norm_gain[None],
         *tables,
     )
-    mixed, grad_inputs, grad_long, short = outs
-    return mixed, grad_inputs, grad_long, short[:, : short_filt.shape[1]]
+    return pl.pallas_call(
+        deliver_kernel,
+        out_shape=(
+            jax.ShapeDtypeStruct((1, block, channels), BF16),
+            jax.ShapeDtypeStruct((3, 1, block, channels), BF16),
+            jax.ShapeDtypeStruct((block, channels), F32),
+            jax.ShapeDtypeStruct(short_filt.shape, F32),
+        ),
+        in_specs=[anywhere] * 4,
+        out_specs=(anywhere,) * 4,
+        scratch_shapes=[
+            pltpu.VMEM((block, channels), BF16),
+            pltpu.VMEM((block, channels), F32),
+            dma((7,)),
+        ],
+        compiler_params=pltpu.CompilerParams(vmem_limit_bytes=60 * 2**20),
+    )(*outs)
 
 
 def operator(q_in, k_in, v_in, short_filt, long_filt, norm_gain, grad_out):

time: 83.1 us -> 107 us (1.29)
  Pallas kernels: 76.9 us -> 106 us
  local copies, waits for them, and re-layouts: 5.4 us -> 0 us
    pallas_call x0 -> x1, Pallas kernels: none -> 35.9 us  [fused(): pl.pallas_call(deliver_kernel, out_shape=(jax.ShapeDtypeStruct((1, block,...]
    pallas_call x1, Pallas kernels: 76.9 us -> 70.5 us  [fused(): pl.pallas_call(functools.partial(operator_kernel, D, lax.axis_size('dp')...]
    unnamed x8 -> x0, local copies, waits for them, and re-layouts: 5.4 us -> none
where the time goes in v3:
time: 107 us
  Pallas kernels  106 us (99%)
    pallas_call x1, Pallas kernels, fused(): pl.pallas_call(functools.partial(operator_kernel, D, lax.axis_size('dp')...  70.5 us
    pallas_call x1, Pallas kernels, fused(): pl.pallas_call(deliver_kernel, out_shape=(jax.ShapeDtypeStruct((1, block,...  35.9 us

profile of v3, /device:TPU:0, one launch (start us, length us, event | category | flops | bytes accessed | tf_op | source)
XLA Modules:
  0.0 107.0 jit_solution(14067296376512480143)
XLA Ops:
  0.6 70.5 %shard_map.138 = (bf16[1,128,1024]{2,1,0:T(8,128)(2,1)}, bf16[3,1,128,1024]{3,2,1,0:T(8,128)(2,1)}, bf16[128,1024]{1,0:T(8,128)(2,1)}, f32[3,7,1024]{2,1,0:T(8,128)}) custom-call(bf16[128,1024]{1,0:T(8,128)(2,1)} %bitcast.5, bf16[128,1024]{1,0:T(8,128)(2,1)} %bitcast.6, bf16[128,1024]{1,0:T(8,128)(2,1)} %bitcast.7, bf16[128,1024]{1,0:T(8,128)(2,1)} %bitcast.8, ...), custom_call_target="tpu_custom_call" | custom-call | tf_op jit(solution)/shard_map/pallas_call | solution.py:672
  71.1 35.9 %shard_map.139 = (bf16[1,128,1024]{2,1,0:T(8,128)(2,1)}, bf16[3,1,128,1024]{3,2,1,0:T(8,128)(2,1)}, f32[128,1024]{1,0:T(8,128)}, f32[3,7,1024]{2,1,0:T(8,128)}) custom-call(bf16[1,128,1024]{2,1,0:T(8,128)(2,1)} %get-tuple-element.8.mixed, bf16[3,1,128,1024]{3,2,1,0:T(8,128)(2,1)} %get-tuple-element.9.grad_inputs, ...), custom_call_target="tpu_custom_call" | custom-call | tf_op jit(solution)/shard_map/pallas_call | solution.py:746

commit v4 on v3

--- a/solution.py
+++ b/solution.py
@@ -209,6 +209,8 @@
     grad_inputs,
     grad_long,
     grad_short,
+    staged,
+    f_staged,
     branch,
     filt,
     wh,
@@ -233,11 +235,13 @@
     dfilt,
     dfilt_in,
     dfilt_sum,
+    long_buf,
     short_sum,
     sent,
     in_send,
     in_recv,
     in_local,
+    stage_sem,
     hop_send,
     hop_recv,
     tab_sem,
@@ -298,6 +302,9 @@
         copy.start()
         return copy
 
+    f_load = local(f_in, f_staged, stage_sem.at[4])
+    loads = {n: local(ref, staged.at[n], stage_sem.at[n]) for n, ref in ((1, k_in), (2, v_in), (0, q_in), (3, g_in))}
+
     barrier = pltpu.get_barrier_semaphore()
     near = [(a, b) for a in range(tens) for b in range(ctx) if a + b > 0]
     for a, b in near:
@@ -310,9 +317,10 @@
     pl.semaphore_signal(barrier, inc=1, device_id=other, device_id_type=MESH)
     pl.semaphore_wait(barrier, len(near) + 1)
 
+    f_load.wait()
     f_copies = [
         remote(
-            f_in.at[:, half_cols(peer(off), dp)],
+            f_staged.at[:, half_cols(peer(off), dp)],
             filt.at[dp, rows_of(me), :],
             in_send.at[4, off],
             in_recv.at[4, off],
@@ -320,13 +328,13 @@
         )
         for off in range(1, ctx)
     ]
-    f_own = local(f_in.at[:, half_cols(me, dp)], filt.at[dp, rows_of(me), :], in_local.at[4])
+    f_own = local(f_staged.at[:, half_cols(me, dp)], filt.at[dp, rows_of(me), :], in_local.at[4])
     land = pl.ds(pl.multiple_of(PAD + me * block, PAD), block)
     arrivals = {}
-    branch_refs = (q_in, k_in, v_in, g_in)
 
     def fetch(n):
-        ref = branch_refs[n]
+        loads[n].wait()
+        ref = staged.at[n]
         arrivals[n] = [
             remote(
                 ref.at[:, cols_of(peer(off))],
@@ -488,14 +496,6 @@
             sums[n, b * 128 : (b + 1) * 128, :] = jnp.broadcast_to(spread[:, b : b + 1], (128, 128))
 
     st_copies = share(0)
-    arrived(3)
-
-    @pl.loop(0, seq // ROWS)
-    def _(i):
-        gz = branch[3, pl.ds(pl.multiple_of(PAD + i * ROWS, PAD), ROWS), :].astype(F32) * gain
-        sums[1, at(i), :] = folded(gz * y_buf[at(i), :])
-
-    prod_copies = share(1)
     inv = 1.0 / jnp.sqrt(gathered(0, st_copies) / model_width + EPS)
     widen(0, inv)
 
@@ -520,6 +520,14 @@
         return copies, local(sent.at[n, rows_of(me), :], target, out_local.at[n])
 
     back = [send_back(3, mixed.at[0, :, cols_of(me)])]
+    arrived(3)
+
+    @pl.loop(0, seq // ROWS)
+    def _(i):
+        gz = branch[3, pl.ds(pl.multiple_of(PAD + i * ROWS, PAD), ROWS), :].astype(F32) * gain
+        sums[1, at(i), :] = folded(gz * y_buf[at(i), :])
+
+    prod_copies = share(1)
     widen(1, gathered(1, prod_copies) * (inv * inv * inv / model_width))
 
     @pl.loop(0, seq // ROWS)
@@ -587,14 +595,14 @@
     gl_copies = [
         remote(
             dfilt_sum.at[rows_of(peer(off)), :],
-            gl_target,
+            long_buf.at[off],
             gl_send.at[off],
             gl_recv.at[off],
             {"context": peer(off)},
         )
         for off in range(1, ctx)
     ]
-    gl_own = local(dfilt_sum.at[rows_of(me), :], gl_target, gl_local)
+    gl_own = [local(dfilt_sum.at[rows_of(me), :], gl_target, gl_local.at[0])]
     forwards = [remote(dfilt_sum.at[rows_of(me), :], gl_target, fw_send.at[0], fw_recv.at[0], other)]
 
     back_short(2)
@@ -606,7 +614,8 @@
     for off in range(1, ctx):
         gl_copies[off - 1].wait_recv()
         piece = grad_long.at[:, half_cols(source(off), dp)]
-        forwards.append(remote(piece, piece, fw_send.at[off], fw_recv.at[off], other))
+        forwards.append(remote(long_buf.at[off], piece, fw_send.at[off], fw_recv.at[off], other))
+        gl_own.append(local(long_buf.at[off], piece, gl_local.at[off]))
     sh_copy.wait_recv()
     short_sum[2] = short_sum[0] + short_sum[1]
     gs_target = grad_short.at[:, :, cols_of(me)]
@@ -619,7 +628,8 @@
         own.wait()
         for copy in copies:
             copy.wait()
-    gl_own.wait()
+    for copy in gl_own:
+        copy.wait()
     for copy in gl_copies:
         copy.wait_send()
     for copy in forwards:
@@ -638,24 +648,26 @@
 
 
 def deliver_kernel(
-    mixed, grad_inputs, grad_long, grad_short, mixed_out, inputs_out, long_out, short_out, narrow, wide, sem
+    mixed, grad_inputs, grad_long, grad_short, mixed_out, inputs_out, long_out, short_out, held, narrow, wide, short, sem
 ):
-    load = pltpu.make_async_copy(grad_long, narrow, sem.at[0])
-    load.start()
-    copies = [
-        pltpu.make_async_copy(mixed, mixed_out, sem.at[1]),
-        pltpu.make_async_copy(grad_short, short_out, sem.at[2]),
-    ]
-    for n in range(3):
-        copies.append(pltpu.make_async_copy(grad_inputs.at[n], inputs_out.at[n], sem.at[3 + n]))
-    for copy in copies:
+    def move(n, src, dst):
+        copy = pltpu.make_async_copy(src, dst, sem.at[n])
         copy.start()
-    load.wait()
+        return copy
+
+    loads = [move(0, grad_long, narrow), move(1, mixed.at[0], held.at[0])]
+    loads += [move(2 + n, grad_inputs.at[n, 0], held.at[1 + n]) for n in range(3)]
+    loads.append(move(5, grad_short, short))
+    loads[0].wait()
     wide[...] = narrow[...].astype(F32)
-    store = pltpu.make_async_copy(wide, long_out, sem.at[6])
-    store.start()
-    store.wait()
-    for copy in copies:
+    stores = [move(6, wide, long_out)]
+    targets = [mixed_out.at[0]] + [inputs_out.at[n, 0] for n in range(3)]
+    for n in range(4):
+        loads[1 + n].wait()
+        stores.append(move(7 + n, held.at[n], targets[n]))
+    loads[5].wait()
+    stores.append(move(11, short, short_out))
+    for copy in stores:
         copy.wait()
 
 
@@ -680,6 +692,8 @@
         in_specs=[in_hbm] * 11,
         out_specs=(anywhere,) * 4,
         scratch_shapes=[
+            pltpu.VMEM((4, block, channels), BF16),
+            pltpu.VMEM((block, channels), F32),
             pltpu.VMEM((4, PAD + seq, width), BF16),
             pltpu.VMEM((2, seq, width // 2), F32),
             pltpu.VMEM((2 * seq, seq), BF16),
@@ -704,10 +718,12 @@
             pltpu.VMEM((2, seq, width // 2), F32),
             pltpu.VMEM((seq, width // 2), F32),
             pltpu.VMEM((seq, width // 2), BF16),
+            pltpu.VMEM((ctx, block, width // 2), BF16),
             pltpu.VMEM((3, 3, short_filt.shape[1], width), F32),
             pltpu.VMEM((4, seq, width), BF16),
             dma((5, ctx)),
             dma((5, ctx)),
+            dma((5,)),
             dma((5,)),
             dma,
             dma,
@@ -721,7 +737,7 @@
             dma,
             dma((ctx,)),
             dma((ctx,)),
-            dma,
+            dma((ctx,)),
             dma((ctx,)),
             dma((ctx,)),
             dma,
@@ -754,9 +770,11 @@
         in_specs=[anywhere] * 4,
         out_specs=(anywhere,) * 4,
         scratch_shapes=[
+            pltpu.VMEM((4, block, channels), BF16),
             pltpu.VMEM((block, channels), BF16),
             pltpu.VMEM((block, channels), F32),
-            dma((7,)),
+            pltpu.VMEM(short_filt.shape, F32),
+            dma((12,)),
         ],
         compiler_params=pltpu.CompilerParams(vmem_limit_bytes=60 * 2**20),
     )(*outs)

time: 107 us -> 78.4 us (0.73)
  Pallas kernels: 106 us -> 77.6 us
    pallas_call x1, Pallas kernels: 35.9 us -> 2.25 us  [fused(): pl.pallas_call(deliver_kernel, out_shape=(jax.ShapeDtypeStruct((1, block,...]
    pallas_call x1, Pallas kernels: 70.5 us -> 75.4 us  [fused(): pl.pallas_call(functools.partial(operator_kernel, D, lax.axis_size('dp')...]
where the time goes in v4:
time: 78.4 us; the launch traced here: 78.3 us
  Pallas kernels  77.6 us (99%)
    pallas_call x1, Pallas kernels, fused(): pl.pallas_call(functools.partial(operator_kernel, D, lax.axis_size('dp')...  75.4 us
    pallas_call x1, Pallas kernels, fused(): pl.pallas_call(deliver_kernel, out_shape=(jax.ShapeDtypeStruct((1, block,...  2.25 us

profile of v4, /device:TPU:0, one launch (start us, length us, event | category | flops | bytes accessed | tf_op | source)
XLA Modules:
  0.0 78.3 jit_solution(4532547986624893879)
XLA Ops:
  0.6 75.4 %shard_map.138 = (bf16[1,128,1024]{2,1,0:T(8,128)(2,1)}, bf16[3,1,128,1024]{3,2,1,0:T(8,128)(2,1)}, bf16[128,1024]{1,0:T(8,128)(2,1)}, f32[3,7,1024]{2,1,0:T(8,128)}) custom-call(bf16[128,1024]{1,0:T(8,128)(2,1)} %bitcast.5, bf16[128,1024]{1,0:T(8,128)(2,1)} %bitcast.6, bf16[128,1024]{1,0:T(8,128)(2,1)} %bitcast.7, bf16[128,1024]{1,0:T(8,128)(2,1)} %bitcast.8, ...), custom_call_target="tpu_custom_call" | custom-call | tf_op jit(solution)/shard_map/pallas_call | solution.py:684
  76.0 2.2 %shard_map.139 = (bf16[1,128,1024]{2,1,0:T(8,128)(2,1)}, bf16[3,1,128,1024]{3,2,1,0:T(8,128)(2,1)}, f32[128,1024]{1,0:T(8,128)}, f32[3,7,1024]{2,1,0:T(8,128)}) custom-call(bf16[1,128,1024]{2,1,0:T(8,128)(2,1)} %get-tuple-element.8.mixed, bf16[3,1,128,1024]{3,2,1,0:T(8,128)(2,1)} %get-tuple-element.9.grad_inputs, ...), custom_call_target="tpu_custom_call" | custom-call | tf_op jit(solution)/shard_map/pallas_call | solution.py:762

commit v5 on v4

--- a/solution.py
+++ b/solution.py
@@ -416,17 +416,6 @@
     def _(i):
         shorts[1, at(i), :] = short_conv(1, i, k_taps)
 
-    for copy in tables:
-        copy.wait()
-    f_hop.wait_recv()
-
-    @pl.loop(0, seq // ROWS)
-    def _(i):
-        op_h[at(i), :half], op_l[at(i), :half] = halves(filt[0, at(i), :])
-        op_h[at(i), half:], op_l[at(i), half:] = halves(filt[1, at(i), :])
-
-    forward(spec_f)
-
     arrived(2)
     fetch(3)
     v_taps = taps_of(2)
@@ -437,7 +426,18 @@
         shorts[2, at(i), :] = vs
         op_h[at(i), :], op_l[at(i), :] = halves(shorts[1, at(i), :] * vs)
 
+    for copy in tables:
+        copy.wait()
     forward(spec_kv)
+
+    f_hop.wait_recv()
+
+    @pl.loop(0, seq // ROWS)
+    def _(i):
+        op_h[at(i), :half], op_l[at(i), :half] = halves(filt[0, at(i), :])
+        op_h[at(i), half:], op_l[at(i), half:] = halves(filt[1, at(i), :])
+
+    forward(spec_f)
     multiply(spec_kv, spec_f, 1.0)
 
     def store_conv(rows, values):
@@ -496,6 +496,14 @@
             sums[n, b * 128 : (b + 1) * 128, :] = jnp.broadcast_to(spread[:, b : b + 1], (128, 128))
 
     st_copies = share(0)
+    arrived(3)
+
+    @pl.loop(0, seq // ROWS)
+    def _(i):
+        gz = branch[3, pl.ds(pl.multiple_of(PAD + i * ROWS, PAD), ROWS), :].astype(F32) * gain
+        sums[1, at(i), :] = folded(gz * y_buf[at(i), :])
+
+    prod_copies = share(1)
     inv = 1.0 / jnp.sqrt(gathered(0, st_copies) / model_width + EPS)
     widen(0, inv)
 
@@ -520,14 +528,6 @@
         return copies, local(sent.at[n, rows_of(me), :], target, out_local.at[n])
 
     back = [send_back(3, mixed.at[0, :, cols_of(me)])]
-    arrived(3)
-
-    @pl.loop(0, seq // ROWS)
-    def _(i):
-        gz = branch[3, pl.ds(pl.multiple_of(PAD + i * ROWS, PAD), ROWS), :].astype(F32) * gain
-        sums[1, at(i), :] = folded(gz * y_buf[at(i), :])
-
-    prod_copies = share(1)
     widen(1, gathered(1, prod_copies) * (inv * inv * inv / model_width))
 
     @pl.loop(0, seq // ROWS)

time: 78.4 us -> 73.8 us (0.941)
  Pallas kernels: 77.6 us -> 73 us
    pallas_call x1, Pallas kernels: 75.4 us -> 70.8 us  [fused(): pl.pallas_call(functools.partial(operator_kernel, D, lax.axis_size('dp')...]
where the time goes in v5:
time: 73.8 us; the launch traced here: 73.6 us
  Pallas kernels  73 us (99%)
    pallas_call x1, Pallas kernels, fused(): pl.pallas_call(functools.partial(operator_kernel, D, lax.axis_size('dp')...  70.8 us
    pallas_call x1, Pallas kernels, fused(): pl.pallas_call(deliver_kernel, out_shape=(jax.ShapeDtypeStruct((1, block,...  2.25 us

profile of v5, /device:TPU:0, one launch (start us, length us, event | category | flops | bytes accessed | tf_op | source)
XLA Modules:
  0.0 73.6 jit_solution(15883756459535431040)
XLA Ops:
  0.6 70.8 %shard_map.138 = (bf16[1,128,1024]{2,1,0:T(8,128)(2,1)}, bf16[3,1,128,1024]{3,2,1,0:T(8,128)(2,1)}, bf16[128,1024]{1,0:T(8,128)(2,1)}, f32[3,7,1024]{2,1,0:T(8,128)}) custom-call(bf16[128,1024]{1,0:T(8,128)(2,1)} %bitcast.5, bf16[128,1024]{1,0:T(8,128)(2,1)} %bitcast.6, bf16[128,1024]{1,0:T(8,128)(2,1)} %bitcast.7, bf16[128,1024]{1,0:T(8,128)(2,1)} %bitcast.8, ...), custom_call_target="tpu_custom_call" | custom-call | tf_op jit(solution)/shard_map/pallas_call | solution.py:684
  71.4 2.2 %shard_map.139 = (bf16[1,128,1024]{2,1,0:T(8,128)(2,1)}, bf16[3,1,128,1024]{3,2,1,0:T(8,128)(2,1)}, f32[128,1024]{1,0:T(8,128)}, f32[3,7,1024]{2,1,0:T(8,128)}) custom-call(bf16[1,128,1024]{2,1,0:T(8,128)(2,1)} %get-tuple-element.8.mixed, bf16[3,1,128,1024]{3,2,1,0:T(8,128)(2,1)} %get-tuple-element.9.grad_inputs, ...), custom_call_target="tpu_custom_call" | custom-call | tf_op jit(solution)/shard_map/pallas_call | solution.py:762

commit v6 on v5

--- a/solution.py
+++ b/solution.py
@@ -174,7 +174,9 @@
 def odd_tables(seq):
     freq = 2 * np.arange(seq)[:, None] + 1
     angle = (freq * np.arange(seq)[None, :] % (4 * seq)) * (np.pi / (2 * seq))
-    forward = np.concatenate([np.cos(angle), -np.sin(angle)], 0)
+    groups = (seq // 128, 1, 128, seq)
+    forward = np.concatenate([np.cos(angle).reshape(groups), -np.sin(angle).reshape(groups)], 1)
+    forward = forward.reshape(2 * seq, seq)
     return split_table(forward) + split_table(np.ascontiguousarray(forward.T) / seq)
 
 
@@ -224,7 +226,6 @@
     op_l,
     spec_kv,
     spec_f,
-    spec_g,
     prod_h,
     prod_l,
     conv,
@@ -380,27 +381,23 @@
             total = total + weights[j] * piece[PAD - j : PAD - j + ROWS]
         return total
 
-    def forward(spec):
-        @pl.loop(0, 2 * seq // 256)
+    def forward(use):
+        @pl.loop(0, 2 * seq // 256, unroll=True)
         def _(m):
             rows = at(m, 256)
-            spec[rows, :] = dot3(wh[rows, :], wl[rows, :], op_h[...], op_l[...])
-
-    def inverse(store):
-        @pl.loop(0, seq // 256)
+            use(rows, dot3(wh[rows, :], wl[rows, :], op_h[...], op_l[...]))
+
+    def inverse(n, store):
+        @pl.loop(0, seq // 256, unroll=True)
         def _(m):
             rows = at(m, 256)
-            store(rows, dot3(vh[rows, :], vl[rows, :], prod_h[...], prod_l[...]))
-
-    def multiply(left, right, sign):
-        @pl.loop(0, seq // ROWS)
-        def _(i):
-            re = at(i)
-            im = pl.ds(pl.multiple_of(seq + i * ROWS, ROWS), ROWS)
-            a, b = left[re, :], left[im, :] * sign
-            c, d = right[re, :], right[im, :]
-            prod_h[re, :], prod_l[re, :] = halves(a * c - b * d)
-            prod_h[im, :], prod_l[im, :] = halves(a * d + b * c)
+            store(rows, dot3(vh[rows, :], vl[rows, :], prod_h[n], prod_l[n]))
+
+    def multiply(n, rows, left, right, sign):
+        a, b = left[:128], left[128:] * sign
+        c, d = right[:128], right[128:]
+        prod = jnp.concatenate([a * c - b * d, a * d + b * c], 0)
+        prod_h[n, rows, :], prod_l[n, rows, :] = halves(prod)
 
     for copy in f_copies:
         copy.wait_recv()
@@ -412,7 +409,7 @@
     fetch(0)
     k_taps = taps_of(1)
 
-    @pl.loop(0, seq // ROWS)
+    @pl.loop(0, seq // ROWS, unroll=2)
     def _(i):
         shorts[1, at(i), :] = short_conv(1, i, k_taps)
 
@@ -420,7 +417,7 @@
     fetch(3)
     v_taps = taps_of(2)
 
-    @pl.loop(0, seq // ROWS)
+    @pl.loop(0, seq // ROWS, unroll=2)
     def _(i):
         vs = short_conv(2, i, v_taps)
         shorts[2, at(i), :] = vs
@@ -428,22 +425,29 @@
 
     for copy in tables:
         copy.wait()
-    forward(spec_kv)
+
+    def keep_kv(rows, values):
+        spec_kv[rows, :] = values
+
+    forward(keep_kv)
 
     f_hop.wait_recv()
 
-    @pl.loop(0, seq // ROWS)
+    @pl.loop(0, seq // ROWS, unroll=2)
     def _(i):
         op_h[at(i), :half], op_l[at(i), :half] = halves(filt[0, at(i), :])
         op_h[at(i), half:], op_l[at(i), half:] = halves(filt[1, at(i), :])
 
-    forward(spec_f)
-    multiply(spec_kv, spec_f, 1.0)
+    def keep_f(rows, values):
+        spec_f[rows, :] = values
+        multiply(0, rows, spec_kv[rows, :], values, 1.0)
+
+    forward(keep_f)
 
     def store_conv(rows, values):
         conv[rows, :] = values
 
-    inverse(store_conv)
+    inverse(0, store_conv)
 
     arrived(0)
     q_taps = taps_of(0)
@@ -454,7 +458,7 @@
             total = total + values[:, n * 128 : (n + 1) * 128]
         return total
 
-    @pl.loop(0, seq // ROWS)
+    @pl.loop(0, seq // ROWS, unroll=2)
     def _(i):
         qs = short_conv(0, i, q_taps)
         shorts[0, at(i), :] = qs
@@ -498,7 +502,7 @@
     st_copies = share(0)
     arrived(3)
 
-    @pl.loop(0, seq // ROWS)
+    @pl.loop(0, seq // ROWS, unroll=2)
     def _(i):
         gz = branch[3, pl.ds(pl.multiple_of(PAD + i * ROWS, PAD), ROWS), :].astype(F32) * gain
         sums[1, at(i), :] = folded(gz * y_buf[at(i), :])
@@ -510,7 +514,7 @@
     def wide(n, i):
         return jnp.concatenate([sums[n, at(i), :]] * (width // 128), 1)
 
-    @pl.loop(0, seq // ROWS)
+    @pl.loop(0, seq // ROWS, unroll=2)
     def _(i):
         sent[3, at(i), :] = (y_buf[at(i), :] * wide(0, i) * gain).astype(BF16)
 
@@ -530,7 +534,7 @@
     back = [send_back(3, mixed.at[0, :, cols_of(me)])]
     widen(1, gathered(1, prod_copies) * (inv * inv * inv / model_width))
 
-    @pl.loop(0, seq // ROWS)
+    @pl.loop(0, seq // ROWS, unroll=2)
     def _(i):
         gz = branch[3, pl.ds(pl.multiple_of(PAD + i * ROWS, PAD), ROWS), :].astype(F32) * gain
         dy = gz * wide(0, i) - y_buf[at(i), :] * wide(1, i)
@@ -542,7 +546,7 @@
     def back_short(n):
         weights = taps_of(n)
 
-        @pl.loop(0, seq // ROWS)
+        @pl.loop(0, seq // ROWS, unroll=2)
         def _(i):
             piece = grads[n, pl.ds(pl.multiple_of(i * ROWS, ROWS), ROWS + 8), :]
             total = weights[0] * piece[:ROWS]
@@ -571,23 +575,24 @@
 
     back_short(0)
 
-    forward(spec_g)
-    multiply(spec_kv, spec_g, -1.0)
+    def use_g(rows, values):
+        multiply(0, rows, spec_kv[rows, :], values, -1.0)
+        multiply(1, rows, spec_f[rows, :], values, -1.0)
+
+    forward(use_g)
 
     def store_dfilt(rows, values):
         dfilt[0, rows, :] = values[:, :half] * scale
         dfilt[1, rows, :] = values[:, half:] * scale
 
-    inverse(store_dfilt)
+    inverse(0, store_dfilt)
     df_copy = remote(dfilt.at[1 - dp], dfilt_in, df_send, df_recv, other)
-
-    multiply(spec_f, spec_g, -1.0)
 
     def store_dkv(rows, values):
         grads[1, rows, :] = values * shorts[2, rows, :]
         grads[2, rows, :] = values * shorts[1, rows, :]
 
-    inverse(store_dkv)
+    inverse(1, store_dkv)
     back_short(1)
     df_copy.wait_recv()
     dfilt_sum[...] = (dfilt[dp] + dfilt_in[...]).astype(BF16)
@@ -707,9 +712,8 @@
             pltpu.VMEM((seq, width), BF16),
             pltpu.VMEM((2 * seq, width), F32),
             pltpu.VMEM((2 * seq, width), F32),
-            pltpu.VMEM((2 * seq, width), F32),
-            pltpu.VMEM((2 * seq, width), BF16),
-            pltpu.VMEM((2 * seq, width), BF16),
+            pltpu.VMEM((2, 2 * seq, width), BF16),
+            pltpu.VMEM((2, 2 * seq, width), BF16),
             pltpu.VMEM((seq, width), F32),
             pltpu.VMEM((seq, width), F32),
             pltpu.VMEM((2, seq, 128), F32),

time: 73.8 us -> 73.2 us (level)
  no operation moved by 1% of the time
where the time goes in v6:
time: 73.2 us; the launch traced here: 73 us
  Pallas kernels  72.4 us (99%)
    pallas_call x1, Pallas kernels, fused(): pl.pallas_call(functools.partial(operator_kernel, D, lax.axis_size('dp')...  70.2 us
    pallas_call x1, Pallas kernels, fused(): pl.pallas_call(deliver_kernel, out_shape=(jax.ShapeDtypeStruct((1, block,...  2.25 us

profile of v6, /device:TPU:0, one launch (start us, length us, event | category | flops | bytes accessed | tf_op | source)
XLA Modules:
  0.0 73.0 jit_solution(2047300616751467669)
XLA Ops:
  0.6 70.2 %shard_map.138 = (bf16[1,128,1024]{2,1,0:T(8,128)(2,1)}, bf16[3,1,128,1024]{3,2,1,0:T(8,128)(2,1)}, bf16[128,1024]{1,0:T(8,128)(2,1)}, f32[3,7,1024]{2,1,0:T(8,128)}) custom-call(bf16[128,1024]{1,0:T(8,128)(2,1)} %bitcast.5, bf16[128,1024]{1,0:T(8,128)(2,1)} %bitcast.6, bf16[128,1024]{1,0:T(8,128)(2,1)} %bitcast.7, bf16[128,1024]{1,0:T(8,128)(2,1)} %bitcast.8, ...), custom_call_target="tpu_custom_call" | custom-call | tf_op jit(solution)/shard_map/pallas_call | solution.py:689
  70.8 2.2 %shard_map.139 = (bf16[1,128,1024]{2,1,0:T(8,128)(2,1)}, bf16[3,1,128,1024]{3,2,1,0:T(8,128)(2,1)}, f32[128,1024]{1,0:T(8,128)}, f32[3,7,1024]{2,1,0:T(8,128)}) custom-call(bf16[1,128,1024]{2,1,0:T(8,128)(2,1)} %get-tuple-element.8.mixed, bf16[3,1,128,1024]{3,2,1,0:T(8,128)(2,1)} %get-tuple-element.9.grad_inputs, ...), custom_call_target="tpu_custom_call" | custom-call | tf_op jit(solution)/shard_map/pallas_call | solution.py:766

commit v7 on v6

--- a/solution.py
+++ b/solution.py
@@ -276,11 +276,16 @@
     taps = short_filt.shape[1]
     other = {"dp": 1 - dp}
 
-    def peer(off):
-        return lax.rem(me + off, ctx)
-
-    def source(off):
-        return lax.rem(me + ctx - off, ctx)
+    steps = (2, 3, 1)
+
+    def peer(step):
+        if step == 1:
+            return me + 1 - 2 * (me % 2)
+        if step == 2:
+            return lax.rem(me + 2, ctx)
+        return 3 - me if step == 3 else me
+
+    source = peer
 
     def rows_of(p):
         return pl.ds(pl.multiple_of(p * block, block), block)
@@ -327,7 +332,7 @@
             in_recv.at[4, off],
             {"context": peer(off)},
         )
-        for off in range(1, ctx)
+        for off in steps
     ]
     f_own = local(f_staged.at[:, half_cols(me, dp)], filt.at[dp, rows_of(me), :], in_local.at[4])
     land = pl.ds(pl.multiple_of(PAD + me * block, PAD), block)
@@ -344,11 +349,12 @@
                 in_recv.at[n, off],
                 {"context": peer(off)},
             )
-            for off in range(1, ctx)
+            for off in steps
         ]
         arrivals[n].append(local(ref.at[:, cols_of(me)], branch.at[n, land, :], in_local.at[n]))
 
     fetch(1)
+    fetch(2)
     small = [local(short_in, short_filt, tab_sem.at[4]), local(gains_in, gain_in, tab_sem.at[5])]
     tables = [
         local(src, dst, tab_sem.at[n])
@@ -403,10 +409,10 @@
         copy.wait_recv()
     f_own.wait()
     f_hop = remote(filt.at[dp], filt.at[dp], hop_send, hop_recv, other)
-    fetch(2)
+    fetch(0)
 
     arrived(1)
-    fetch(0)
+    fetch(3)
     k_taps = taps_of(1)
 
     @pl.loop(0, seq // ROWS, unroll=2)
@@ -414,7 +420,6 @@
         shorts[1, at(i), :] = short_conv(1, i, k_taps)
 
     arrived(2)
-    fetch(3)
     v_taps = taps_of(2)
 
     @pl.loop(0, seq // ROWS, unroll=2)
@@ -527,7 +532,7 @@
                 out_recv.at[n, off],
                 {"context": peer(off)},
             )
-            for off in range(1, ctx)
+            for off in steps
         ]
         return copies, local(sent.at[n, rows_of(me), :], target, out_local.at[n])
 
@@ -605,7 +610,7 @@
             gl_recv.at[off],
             {"context": peer(off)},
         )
-        for off in range(1, ctx)
+        for off in steps
     ]
     gl_own = [local(dfilt_sum.at[rows_of(me), :], gl_target, gl_local.at[0])]
     forwards = [remote(dfilt_sum.at[rows_of(me), :], gl_target, fw_send.at[0], fw_recv.at[0], other)]
@@ -616,8 +621,8 @@
         short_grads(n)
     sh_copy = remote(short_sum.at[0], short_sum.at[1], sh_send, sh_recv, other)
 
-    for off in range(1, ctx):
-        gl_copies[off - 1].wait_recv()
+    for off in steps:
+        gl_copies[steps.index(off)].wait_recv()
         piece = grad_long.at[:, half_cols(source(off), dp)]
         forwards.append(remote(long_buf.at[off], piece, fw_send.at[off], fw_recv.at[off], other))
         gl_own.append(local(long_buf.at[off], piece, gl_local.at[off]))
@@ -626,7 +631,7 @@
     gs_target = grad_short.at[:, :, cols_of(me)]
     gs_copies = [
         remote(short_sum.at[2], gs_target, gs_send.at[off], gs_recv.at[off], {"context": peer(off)})
-        for off in range(1, ctx)
+        for off in steps
     ]
     gs_own = local(short_sum.at[2], gs_target, gs_local)
     for copies, own in back:
@@ -788,7 +793,7 @@
     _, block, channels = q_in.shape
     ctx = lax.axis_size("context")
     dense = block * ctx <= 1024 and block % 128 == 0 and channels % (256 * ctx) == 0
-    form = fused if dense and lax.axis_size("dp") == 2 else shards
+    form = fused if dense and lax.axis_size("dp") == 2 and ctx == 4 else shards
     return form(q_in, k_in, v_in, short_filt, long_filt, norm_gain, grad_out)
 
 

time: 73.2 us -> 73.1 us (level)
  no operation moved by 1% of the time
where the time goes in v7:
time: 73.1 us; the launch traced here: 73 us
  Pallas kernels  72.3 us (99%)
    pallas_call x1, Pallas kernels, fused(): pl.pallas_call(functools.partial(operator_kernel, D, lax.axis_size('dp')...  70.1 us
    pallas_call x1, Pallas kernels, fused(): pl.pallas_call(deliver_kernel, out_shape=(jax.ShapeDtypeStruct((1, block,...  2.25 us

profile of v7, /device:TPU:0, one launch (start us, length us, event | category | flops | bytes accessed | tf_op | source)
XLA Modules:
  0.0 73.0 jit_solution(14080395289818877733)
XLA Ops:
  0.6 70.1 %shard_map.138 = (bf16[1,128,1024]{2,1,0:T(8,128)(2,1)}, bf16[3,1,128,1024]{3,2,1,0:T(8,128)(2,1)}, bf16[128,1024]{1,0:T(8,128)(2,1)}, f32[3,7,1024]{2,1,0:T(8,128)}) custom-call(bf16[128,1024]{1,0:T(8,128)(2,1)} %bitcast.5, bf16[128,1024]{1,0:T(8,128)(2,1)} %bitcast.6, bf16[128,1024]{1,0:T(8,128)(2,1)} %bitcast.7, bf16[128,1024]{1,0:T(8,128)(2,1)} %bitcast.8, ...), custom_call_target="tpu_custom_call" | custom-call | tf_op jit(solution)/shard_map/pallas_call | solution.py:694
  70.7 2.2 %shard_map.139 = (bf16[1,128,1024]{2,1,0:T(8,128)(2,1)}, bf16[3,1,128,1024]{3,2,1,0:T(8,128)(2,1)}, f32[128,1024]{1,0:T(8,128)}, f32[3,7,1024]{2,1,0:T(8,128)}) custom-call(bf16[1,128,1024]{2,1,0:T(8,128)(2,1)} %get-tuple-element.8.mixed, bf16[3,1,128,1024]{3,2,1,0:T(8,128)(2,1)} %get-tuple-element.9.grad_inputs, ...), custom_call_target="tpu_custom_call" | custom-call | tf_op jit(solution)/shard_map/pallas_call | solution.py:771

commit v8 on v7

--- a/solution.py
+++ b/solution.py
@@ -599,6 +599,8 @@
 
     inverse(1, store_dkv)
     back_short(1)
+    back_short(2)
+    short_grads(0)
     df_copy.wait_recv()
     dfilt_sum[...] = (dfilt[dp] + dfilt_in[...]).astype(BF16)
     gl_target = grad_long.at[:, half_cols(me, dp)]
@@ -615,9 +617,7 @@
     gl_own = [local(dfilt_sum.at[rows_of(me), :], gl_target, gl_local.at[0])]
     forwards = [remote(dfilt_sum.at[rows_of(me), :], gl_target, fw_send.at[0], fw_recv.at[0], other)]
 
-    back_short(2)
-
-    for n in range(3):
+    for n in (1, 2):
         short_grads(n)
     sh_copy = remote(short_sum.at[0], short_sum.at[1], sh_send, sh_recv, other)
 

time: 73.1 us -> 75 us (1.026)
  Pallas kernels: 72.3 us -> 74.3 us
    pallas_call x1, Pallas kernels: 70.1 us -> 72 us  [fused(): pl.pallas_call(functools.partial(operator_kernel, D, lax.axis_size('dp')...]
where the time goes in v8:
time: 75 us; the launch traced here: 74.9 us
  Pallas kernels  74.3 us (99%)
    pallas_call x1, Pallas kernels, fused(): pl.pallas_call(functools.partial(operator_kernel, D, lax.axis_size('dp')...  72 us
    pallas_call x1, Pallas kernels, fused(): pl.pallas_call(deliver_kernel, out_shape=(jax.ShapeDtypeStruct((1, block,...  2.25 us

profile of v8, /device:TPU:0, one launch (start us, length us, event | category | flops | bytes accessed | tf_op | source)
XLA Modules:
  0.0 74.9 jit_solution(12396513786426580516)
XLA Ops:
  0.6 72.0 %shard_map.138 = (bf16[1,128,1024]{2,1,0:T(8,128)(2,1)}, bf16[3,1,128,1024]{3,2,1,0:T(8,128)(2,1)}, bf16[128,1024]{1,0:T(8,128)(2,1)}, f32[3,7,1024]{2,1,0:T(8,128)}) custom-call(bf16[128,1024]{1,0:T(8,128)(2,1)} %bitcast.5, bf16[128,1024]{1,0:T(8,128)(2,1)} %bitcast.6, bf16[128,1024]{1,0:T(8,128)(2,1)} %bitcast.7, bf16[128,1024]{1,0:T(8,128)(2,1)} %bitcast.8, ...), custom_call_target="tpu_custom_call" | custom-call | tf_op jit(solution)/shard_map/pallas_call | solution.py:694
  72.6 2.2 %shard_map.139 = (bf16[1,128,1024]{2,1,0:T(8,128)(2,1)}, bf16[3,1,128,1024]{3,2,1,0:T(8,128)(2,1)}, f32[128,1024]{1,0:T(8,128)}, f32[3,7,1024]{2,1,0:T(8,128)}) custom-call(bf16[1,128,1024]{2,1,0:T(8,128)(2,1)} %get-tuple-element.8.mixed, bf16[3,1,128,1024]{3,2,1,0:T(8,128)(2,1)} %get-tuple-element.9.grad_inputs, ...), custom_call_target="tpu_custom_call" | custom-call | tf_op jit(solution)/shard_map/pallas_call | solution.py:771
